TPU v7x, 512 devices: a whole 4x8x8 slice. The times are simulated.
512 devices in a mesh: lat: 32 (over z_hi, y, core), chan: 4 (over z_lo), tm: 4 (over x).
Axes of the slice: x: 4, y: 8, z: 8 (z_hi: 2, z_lo: 4; z = z_hi * 4 + z_lo), core: 2. Of those that a mesh axis runs over, the one named last changes fastest.
Arguments:
- fields: bfloat16 [512, 1440, 256], P(('tm', 'lat'), None, 'chan'), parts along dimension 0, may hold values from -6 to 6
- disco_weight: bfloat16 [6, 256, 64], P(None, 'chan'), may hold values from -0.25 to 0.25
- support_lat: int32 [128, 9], P('lat'), may hold values from -2 to 2
- support_lon: int32 [128, 9], P('lat'), may hold values from -4 to 4
- support_basis: int32 [128, 9], P('lat'), may hold values from 0 to 5
- support_value: float32 [128, 9], P('lat'), may hold values from 0.25 to 1.5
- w_up: bfloat16 [256, 512], replicated, may hold values from -0.375 to 0.375
- w_down: bfloat16 [512, 256], replicated, may hold values from -0.25 to 0.25
- legendre: bfloat16 [384, 384, 128], P(('lat', 'chan')), may hold values from -0.5 to 0.5
Outputs:
- coefficients: bfloat16 [1536, 384, 512], P(('tm', 'lat', 'chan')), parts along dimension 0
There are 4 independent parts, one for each index of `tm`. A program takes and returns all parts, laid end to end along the dimension named above; an argument that names none is the same for every part. Nothing has to cross between parts.
All inputs are finite; a program needn't handle non-finite values.
Results may differ from a plain program's by a relative error of at most 0.0076.
Values may be sent and summed in bfloat16 or wider, within the bound.
A program may use at most 128 MiB of HBM per device.

v0:
```python
import math

import jax
import jax.numpy as jnp
from jax import lax
from jax.sharding import PartitionSpec as P

G = 64
NB = 6
S = 9
HALO = 2
DLON = 4


def with_halo(cells, sides, width):
    for axis, dim in sides:
        count = lax.axis_size(axis)
        ends = count - 1
        head = lax.slice_in_dim(cells, 0, width, axis=dim)
        tail = lax.slice_in_dim(cells, cells.shape[dim] - width, cells.shape[dim], axis=dim)
        cells = jnp.concatenate(
            [
                lax.ppermute(tail, axis, [(i, (i + 1) % count) for i in range(ends)]),
                cells,
                lax.ppermute(head, axis, [((i + 1) % count, i) for i in range(ends)]),
            ],
            axis=dim,
        )
    return cells


def fourier_table(lon_count, mode_count):
    lon_index = jnp.arange(lon_count, dtype=jnp.int32)
    mode_index = jnp.arange(mode_count, dtype=jnp.int32)
    phase = lon_index[:, None] * mode_index[None, :] % lon_count
    angle = phase.astype(jnp.float32) * (2.0 * math.pi / lon_count)
    paired = jnp.stack([jnp.cos(angle), -jnp.sin(angle)], axis=-1) * math.sqrt(2.0 / lon_count)
    return paired.reshape(lon_count, 2 * mode_count).astype(jnp.bfloat16)


def channel_mlp(row_block, w_up, w_down):
    values = row_block.astype(jnp.float32)
    center = values - jnp.mean(values, axis=-1, keepdims=True)
    spread = jnp.mean(center * center, axis=-1, keepdims=True)
    normed = (center * lax.rsqrt(spread + 1e-05)).astype(jnp.bfloat16)
    lifted = jnp.einsum("anc,ch->anh", normed, w_up, preferred_element_type=jnp.float32)
    active = jax.nn.gelu(lifted).astype(jnp.bfloat16)
    lowered = jnp.einsum("anh,hc->anc", active, w_down, preferred_element_type=jnp.float32)
    return (values + lowered).astype(jnp.bfloat16)


def on_device(
    fields,
    disco_weight,
    support_lat,
    support_lon,
    support_basis,
    support_value,
    w_up,
    w_down,
    legendre,
):
    lat_dev, lon_count, chans_dev = fields.shape
    group_count = chans_dev // G
    num_lat = lax.axis_size("lat")
    num_chan = lax.axis_size("chan")
    mode_dev = legendre.shape[0]
    degree_count = legendre.shape[1]
    mode_count = mode_dev * num_lat * num_chan
    padded = with_halo(fields, (("lat", 0),), HALO)
    wrapped = jnp.concatenate([padded[:, lon_count - DLON :], padded, padded[:, :DLON]], axis=1)
    row_ids = jnp.arange(lat_dev, dtype=jnp.int32)
    onehot = (support_basis[:, :, None] == jnp.arange(NB, dtype=jnp.int32)[None, None, :]).astype(
        jnp.float32
    )
    flat_weight = disco_weight.astype(jnp.float32).reshape(NB, chans_dev * G)
    picked = jnp.einsum("asb,bk->ask", onehot, flat_weight, precision=lax.Precision.HIGHEST)
    filters = (
        (picked * support_value[:, :, None])
        .astype(jnp.bfloat16)
        .reshape(lat_dev, S, group_count, G, G)
    )

    def shift_row(source_row, start):
        return lax.dynamic_slice(wrapped, (source_row, start, 0), (1, lon_count, chans_dev))[0]

    accumulated = jnp.zeros((lat_dev, lon_count, group_count, G), jnp.float32)
    for position in range(S):
        source = row_ids + HALO + support_lat[:, position]
        starts = DLON + support_lon[:, position]
        slab = jax.vmap(shift_row)(source, starts).reshape(lat_dev, lon_count, group_count, G)
        accumulated = accumulated + jnp.einsum(
            "anhi,ahoi->anho", slab, filters[:, position], preferred_element_type=jnp.float32
        )
    accumulated = accumulated.reshape(lat_dev, lon_count, chans_dev)
    mixed = (fields.astype(jnp.float32) + accumulated).astype(jnp.bfloat16)
    fourier = fourier_table(lon_count, mode_count)
    mode_start = lax.axis_index(("lat", "chan")) * mode_dev
    mode_ids = mode_start + jnp.arange(mode_dev, dtype=jnp.int32)
    degree = jnp.arange(degree_count, dtype=jnp.int32)
    kept_mask = degree[None, :] >= mode_ids[:, None]
    kept = jnp.where(kept_mask[:, :, None], legendre, jnp.zeros((), jnp.bfloat16))
    mixed_rows = channel_mlp(
        lax.all_to_all(mixed, "chan", split_axis=0, concat_axis=2, tiled=True), w_up, w_down
    )
    banded = lax.all_to_all(mixed_rows, "chan", split_axis=2, concat_axis=0, tiled=True)
    spectrum = jnp.einsum("anc,nk->akc", banded, fourier, preferred_element_type=jnp.float32)
    spectrum = spectrum.astype(jnp.bfloat16).reshape(lat_dev, mode_count, 2 * chans_dev)
    gathered_modes = lax.all_to_all(
        lax.all_to_all(spectrum, "lat", split_axis=1, concat_axis=0, tiled=True),
        "chan",
        split_axis=1,
        concat_axis=0,
        tiled=True,
    )
    gathered_modes = gathered_modes.reshape(num_chan, -1, mode_dev, 2 * chans_dev)
    coefficients = jnp.einsum(
        "mla,jamk->mljk", kept, gathered_modes, preferred_element_type=jnp.float32
    )
    coefficients = coefficients.reshape(mode_dev, degree_count, num_chan, 2, chans_dev)
    coefficients = jnp.transpose(coefficients, (0, 1, 3, 2, 4)).reshape(mode_dev, degree_count, -1)
    return coefficients.astype(jnp.bfloat16)


def solution(mesh):
    in_specs = (
        P(("tm", "lat"), None, "chan"),
        P(None, "chan", None),
        P("lat", None),
        P("lat", None),
        P("lat", None),
        P("lat", None),
        P(),
        P(),
        P(("lat", "chan"), None, None),
    )
    out_specs = P(("tm", "lat", "chan"), None, None)
    return jax.shard_map(
        on_device, mesh=mesh, in_specs=in_specs, out_specs=out_specs, check_vma=False
    )
```

profile of v0, /device:TPU:1, one launch (start us, length us, event | category | flops | bytes accessed | tf_op | source)
XLA Modules:
  0.0 273.0 jit_solution(6160790855536458580)
XLA Ops:
  0.0 2.0 fusion.60
  2.0 8.9 %collective-permute-start.1 = (bf16[2,1440,64]{1,2,0:T(8,128)(2,1)}, bf16[2,1440,64]{1,2,0:T(8,128)(2,1)S(1)}, u32[]{:S(2)}, u32[]{:S(2)}) collective-permute-start(bf16[2,1440,64]{1,2,0:T(8,128)(2,1)} %get-tuple-element.170), channel_id=1, source_target_pairs={{16,0},{32,16},{48,32},{64,48},{80,64},{96,80},{112,96},{128,112},... | collective-permute-start | bytes 1105928 | tf_op jit(solution)/shard_map/ppermute | solution.py:25
  10.9 1.9 collective-permute-start
  21.2 13.7 %concatenate.34 = bf16[8,1448,64]{2,1,0:T(8,128)(2,1)S(1)} concatenate(bf16[8,4,64]{2,1,0:T(4,128)(2,1)S(1)} %get-tuple-element.168, bf16[8,1440,64]{2,1,0:T(8,128)(2,1)} %copy-done.1, bf16[8,4,64]{2,1,0:T(4,128)(2,1)S(1)} %get-tuple-element.167), dimensions={1} | concatenate | bytes 2965504 | tf_op jit(solution)/shard_map/concatenate | solution.py:71
  36.2 11.2 %while.9 = (s32[]{:T(128)}, bf16[8,1448,64]{2,1,0:T(8,128)(2,1)S(1)}, s32[4,3]{1,0:T(4,128)S(1)}, bf16[4,1,1440,64]{3,2,1,0:T(8,128)(2,1)}, s32[]{:T(128)}) while((s32[]{:T(128)}, bf16[8,1448,64]{2,1,0:T(8,128)(2,1)S(1)}, s32[4,3]{1,0:T(4,128)S(1)}, bf16[4,1,1440,64]{3,2,1,0:T(8,128)(2,1)}, s32[]{:T(128)}) %tuple.166), condition=%wide.while_cond, body=%wide.while_body.sunk | while | flops 2 | bytes 554601 | solution.py:85
  36.9 2.2 bitcast_dynamic-update-slice_fusion.18
  39.7 2.1 bitcast_dynamic-update-slice_fusion.18
  42.5 2.1 bitcast_dynamic-update-slice_fusion.18
  45.3 2.1 bitcast_dynamic-update-slice_fusion.18
  48.7 11.0 %while.10 = (s32[]{:T(128)}, bf16[8,1448,64]{2,1,0:T(8,128)(2,1)S(1)}, s32[4,3]{1,0:T(4,128)S(1)}, bf16[4,1,1440,64]{3,2,1,0:T(8,128)(2,1)}, s32[]{:T(128)}) while((s32[]{:T(128)}, bf16[8,1448,64]{2,1,0:T(8,128)(2,1)S(1)}, s32[4,3]{1,0:T(4,128)S(1)}, bf16[4,1,1440,64]{3,2,1,0:T(8,128)(2,1)}, s32[]{:T(128)}) %tuple.193), condition=%wide.while_cond.1, body=%wide.while_body.1.sunk | while | flops 2 | bytes 554601 | solution.py:85
  49.3 2.1 bitcast_dynamic-update-slice_fusion.19
  52.1 2.1 bitcast_dynamic-update-slice_fusion.19
  54.8 2.1 bitcast_dynamic-update-slice_fusion.19
  57.6 2.1 bitcast_dynamic-update-slice_fusion.19
  61.0 11.0 %while.11 = (s32[]{:T(128)}, bf16[8,1448,64]{2,1,0:T(8,128)(2,1)S(1)}, s32[4,3]{1,0:T(4,128)S(1)}, bf16[4,1,1440,64]{3,2,1,0:T(8,128)(2,1)}, s32[]{:T(128)}) while((s32[]{:T(128)}, bf16[8,1448,64]{2,1,0:T(8,128)(2,1)S(1)}, s32[4,3]{1,0:T(4,128)S(1)}, bf16[4,1,1440,64]{3,2,1,0:T(8,128)(2,1)}, s32[]{:T(128)}) %tuple.194), condition=%wide.while_cond.2, body=%wide.while_body.2.sunk | while | flops 2 | bytes 554601 | solution.py:85
  61.7 2.1 bitcast_dynamic-update-slice_fusion.20
  64.4 2.1 bitcast_dynamic-update-slice_fusion.20
  67.1 2.1 bitcast_dynamic-update-slice_fusion.20
  69.9 2.1 bitcast_dynamic-update-slice_fusion.20
  73.3 11.4 %while.12 = (s32[]{:T(128)}, bf16[8,1448,64]{2,1,0:T(8,128)(2,1)S(1)}, s32[4,3]{1,0:T(4,128)S(1)}, bf16[4,1,1440,64]{3,2,1,0:T(8,128)(2,1)}, s32[]{:T(128)}) while((s32[]{:T(128)}, bf16[8,1448,64]{2,1,0:T(8,128)(2,1)S(1)}, s32[4,3]{1,0:T(4,128)S(1)}, bf16[4,1,1440,64]{3,2,1,0:T(8,128)(2,1)}, s32[]{:T(128)}) %tuple.195), condition=%wide.while_cond.3, body=%wide.while_body.3.sunk | while | flops 2 | bytes 554601 | solution.py:85
  74.0 2.2 bitcast_dynamic-update-slice_fusion.21
  76.9 2.2 bitcast_dynamic-update-slice_fusion.21
  79.7 2.2 bitcast_dynamic-update-slice_fusion.21
  82.6 2.2 bitcast_dynamic-update-slice_fusion.21
  86.1 10.8 %while.13 = (s32[]{:T(128)}, bf16[8,1448,64]{2,1,0:T(8,128)(2,1)S(1)}, s32[4,3]{1,0:T(4,128)S(1)}, bf16[4,1,1440,64]{3,2,1,0:T(8,128)(2,1)}, s32[]{:T(128)}) while((s32[]{:T(128)}, bf16[8,1448,64]{2,1,0:T(8,128)(2,1)S(1)}, s32[4,3]{1,0:T(4,128)S(1)}, bf16[4,1,1440,64]{3,2,1,0:T(8,128)(2,1)}, s32[]{:T(128)}) %tuple.196), condition=%wide.while_cond.4, body=%wide.while_body.4.sunk | while | flops 2 | bytes 554601 | solution.py:85
  86.7 2.1 bitcast_dynamic-update-slice_fusion.22
  89.4 2.1 bitcast_dynamic-update-slice_fusion.22
  92.1 2.1 bitcast_dynamic-update-slice_fusion.22
  94.8 2.1 bitcast_dynamic-update-slice_fusion.22
  98.3 10.3 %while.14 = (s32[]{:T(128)}, bf16[8,1448,64]{2,1,0:T(8,128)(2,1)S(1)}, s32[4,3]{1,0:T(4,128)S(1)}, bf16[4,1,1440,64]{3,2,1,0:T(8,128)(2,1)}, s32[]{:T(128)}) while((s32[]{:T(128)}, bf16[8,1448,64]{2,1,0:T(8,128)(2,1)S(1)}, s32[4,3]{1,0:T(4,128)S(1)}, bf16[4,1,1440,64]{3,2,1,0:T(8,128)(2,1)}, s32[]{:T(128)}) %tuple.197), condition=%wide.while_cond.5, body=%wide.while_body.5.sunk | while | flops 2 | bytes 554601 | solution.py:85
  98.9 2.0 bitcast_dynamic-update-slice_fusion.23
  101.5 2.0 bitcast_dynamic-update-slice_fusion.23
  104.1 2.0 bitcast_dynamic-update-slice_fusion.23
  106.6 2.0 bitcast_dynamic-update-slice_fusion.23
  110.0 10.1 %while.15 = (s32[]{:T(128)}, bf16[8,1448,64]{2,1,0:T(8,128)(2,1)S(1)}, s32[4,3]{1,0:T(4,128)S(1)}, bf16[4,1,1440,64]{3,2,1,0:T(8,128)(2,1)}, s32[]{:T(128)}) while((s32[]{:T(128)}, bf16[8,1448,64]{2,1,0:T(8,128)(2,1)S(1)}, s32[4,3]{1,0:T(4,128)S(1)}, bf16[4,1,1440,64]{3,2,1,0:T(8,128)(2,1)}, s32[]{:T(128)}) %tuple.198), condition=%wide.while_cond.6, body=%wide.while_body.6.sunk | while | flops 2 | bytes 554601 | solution.py:85
  110.5 1.9 bitcast_dynamic-update-slice_fusion.24
  113.0 2.0 bitcast_dynamic-update-slice_fusion.24
  115.5 2.0 bitcast_dynamic-update-slice_fusion.24
  118.1 2.0 bitcast_dynamic-update-slice_fusion.24
  121.3 10.4 %while.16 = (s32[]{:T(128)}, bf16[8,1448,64]{2,1,0:T(8,128)(2,1)S(1)}, s32[4,3]{1,0:T(4,128)S(1)}, bf16[4,1,1440,64]{3,2,1,0:T(8,128)(2,1)}, s32[]{:T(128)}) while((s32[]{:T(128)}, bf16[8,1448,64]{2,1,0:T(8,128)(2,1)S(1)}, s32[4,3]{1,0:T(4,128)S(1)}, bf16[4,1,1440,64]{3,2,1,0:T(8,128)(2,1)}, s32[]{:T(128)}) %tuple.199), condition=%wide.while_cond.7, body=%wide.while_body.7.sunk | while | flops 2 | bytes 554601 | solution.py:85
  121.9 2.0 bitcast_dynamic-update-slice_fusion.25
  124.5 2.0 bitcast_dynamic-update-slice_fusion.25
  127.1 2.0 bitcast_dynamic-update-slice_fusion.25
  129.8 2.0 bitcast_dynamic-update-slice_fusion.25
  133.2 10.9 %while.17 = (s32[]{:T(128)}, bf16[8,1448,64]{2,1,0:T(8,128)(2,1)S(1)}, s32[4,3]{1,0:T(4,128)S(1)}, bf16[4,1,1440,64]{3,2,1,0:T(8,128)(2,1)}, s32[]{:T(128)}) while((s32[]{:T(128)}, bf16[8,1448,64]{2,1,0:T(8,128)(2,1)S(1)}, s32[4,3]{1,0:T(4,128)S(1)}, bf16[4,1,1440,64]{3,2,1,0:T(8,128)(2,1)}, s32[]{:T(128)}) %tuple.200), condition=%wide.while_cond.8, body=%wide.while_body.8.sunk | while | flops 2 | bytes 554601 | solution.py:85
  133.8 2.1 bitcast_dynamic-update-slice_fusion.26
  136.5 2.1 bitcast_dynamic-update-slice_fusion.26
  139.2 2.1 bitcast_dynamic-update-slice_fusion.26
  142.0 2.1 bitcast_dynamic-update-slice_fusion.26
  144.1 2.2 fusion.31
  156.8 22.6 %all_to_all.60 = bf16[4,1440,64]{1,2,0:T(8,128)(2,1)S(1)} all-to-all(bf16[4,1440,64]{1,2,0:T(8,128)(2,1)S(1)} %fusion.12), channel_id=1, replica_groups=mesh['lat'=32,'chan'=4,'tm'=4] {'chan'}, dimensions={0} | all-to-all | bytes 1474560 | tf_op jit(solution)/shard_map/all_to_all | solution.py:104
  180.3 3.2 %fusion.14 = bf16[1,1440,256]{2,1,0:T(8,128)(2,1)} fusion(f32[1440,256]{1,0:T(8,128)S(1)} %copy.119, bf16[512,256]{1,0:T(8,128)(2,1)S(1)} %copy-done, bf16[256,512]{1,0:T(8,128)(2,1)} %param.15, f32[1440,256]{0,1:T(8,128)S(1)} %bitcast.220, f32[1440]{0:T(1024)S(1)} %add_rsqrt_fusion, f32[1440]{0:T(1024)S(1)} %broadcast_multiply_fusion), kind=kOutput, calls=%fused_computation.46 | convolution fusion | flops 763453440 | bytes 4222208 | tf_op jit(solution)/shard_map/anh,hc->anc/dot_general | solution.py:48
  183.5 3.6 %copy.120 = bf16[1,1440,256]{1,0,2:T(2,128)(2,1)S(1)} copy(bf16[1,1440,256]{2,1,0:T(8,128)(2,1)} %fusion.14) | data formatting | bytes 1474560 | tf_op jit(solution)/shard_map/convert_element_type | solution.py:49
  187.6 5.6 %reduce.5 = bf16[256,1440]{1,0:T(8,128)(2,1)S(1)} reduce(bf16[256,1,1440]{2,1,0:T(2,128)(2,1)S(1)} %bitcast.222, bf16[]{:T(256)} %broadcast.411), dimensions={1}, to_apply=%bitcast.156.reduce_sub_computation | reduce | bytes 1474562
  193.3 2.0 reshape.556
  195.3 3.7 %all-to-all-start.1 = ((bf16[4,2,46080]{2,1,0:T(2,128)(2,1)}), bf16[4,2,46080]{2,1,0:T(2,128)(2,1)S(1)}, u32[]{:S(2)}, u32[]{:S(2)}) async-start(bf16[4,2,46080]{2,1,0:T(2,128)(2,1)} %reshape.556), calls=%async_computation.1 | async-start | bytes 1474560 | tf_op jit(solution)/shard_map/all_to_all | solution.py:106
  199.0 9.2 %sine_negate_fusion = (f32[1440,384,1]{1,0,2:T(8,128)S(1)}, f32[1440,384,1]{1,0,2:T(8,128)S(1)}) fusion(), kind=kLoop, calls=%fused_computation.49 | loop fusion | flops 5529600 | bytes 4423680 | tf_op jit(solution)/shard_map/neg | solution.py:37
  208.2 1.8 fusion.1
  210.0 5.9 %copy.96 = bf16[1440,384,2]{0,2,1:T(2,128)(2,1)S(1)} copy(bf16[1440,384,2]{1,0,2:T(8,128)(2,1)} %fusion.1) | data formatting | bytes 4423680 | tf_op jit(solution)/shard_map/convert_element_type | solution.py:38
  215.9 3.0 %convert_element_type.110 = bf16[1440,768]{0,1:T(8,128)(2,1)} reshape(bf16[1440,384,2]{0,2,1:T(2,128)(2,1)S(1)} %copy.96) | data formatting | bytes 4423680 | tf_op jit(solution)/shard_map/convert_element_type | solution.py:38
  220.4 2.5 fusion.33
  223.9 31.9 %all_to_all.61 = bf16[4,384,128]{2,0,1:T(4,128)(2,1)S(1)} all-to-all(bf16[4,384,128]{2,0,1:T(4,128)(2,1)S(1)} %copy.123), channel_id=1, replica_groups=mesh['lat'=32,'chan'=4,'tm'=4] {'lat'}, dimensions={1} | all-to-all | bytes 786432 | tf_op jit(solution)/shard_map/all_to_all | solution.py:110
  256.8 4.6 %all-to-all-start.3 = ((bf16[128,12,128]{2,0,1:T(8,128)(2,1)}), bf16[128,12,128]{2,0,1:T(8,128)(2,1)S(1)}, u32[]{:S(2)}, u32[]{:S(2)}) async-start(bf16[128,12,128]{2,0,1:T(8,128)(2,1)} %bitcast.45), calls=%async_computation.3 | async-start | bytes 786432 | tf_op jit(solution)/shard_map/all_to_all | solution.py:109
  261.4 9.0 %all-to-all-done.3 = bf16[128,12,128]{2,0,1:T(8,128)(2,1)S(1)} async-done(((bf16[128,12,128]{2,0,1:T(8,128)(2,1)}), bf16[128,12,128]{2,0,1:T(8,128)(2,1)S(1)}, u32[]{:S(2)}, u32[]{:S(2)}) %all-to-all-start.3) | async-done | bytes 393248 | tf_op jit(solution)/shard_map/all_to_all | solution.py:109
  (163 shorter events, 60.5 us)
Async XLA Ops:
  0.0 180.3 %copy-start = (bf16[512,256]{1,0:T(8,128)(2,1)S(1)}, bf16[512,256]{1,0:T(8,128)(2,1)}, u32[]{:S(2)}) copy-start(bf16[512,256]{1,0:T(8,128)(2,1)} %param.16) | copy-start | bytes 786436
  0.0 12.9 %copy-start.2 = (bf16[4,1440,64]{1,2,0:T(8,128)(2,1)S(1)}, bf16[4,1440,64]{1,2,0:T(8,128)(2,1)}, u32[]{:S(2)}) copy-start(bf16[4,1440,64]{1,2,0:T(8,128)(2,1)} %param.9) | copy-start | bytes 2211844
  0.0 13.7 %copy-start.16 = (bf16[6,64,64]{2,1,0:T(8,128)(2,1)S(1)}, bf16[6,64,64]{2,1,0:T(8,128)(2,1)}, u32[]{:S(2)}) copy-start(bf16[6,64,64]{2,1,0:T(8,128)(2,1)} %param.10) | copy-start | bytes 147460
  2.0 11.9 %copy-start.17 = (f32[4,9]{1,0:T(4,128)S(1)}, f32[4,9]{1,0:T(4,128)}, u32[]{:S(2)}) copy-start(f32[4,9]{1,0:T(4,128)} %param.14) | copy-start | bytes 436
  2.0 11.9 %copy-start.18 = (s32[4,9]{1,0:T(4,128)S(1)}, s32[4,9]{1,0:T(4,128)}, u32[]{:S(2)}) copy-start(s32[4,9]{1,0:T(4,128)} %param.13) | copy-start | bytes 436
  2.0 14.1 %collective-permute-start.1 = (bf16[2,1440,64]{1,2,0:T(8,128)(2,1)}, bf16[2,1440,64]{1,2,0:T(8,128)(2,1)S(1)}, u32[]{:S(2)}, u32[]{:S(2)}) collective-permute-start(bf16[2,1440,64]{1,2,0:T(8,128)(2,1)} %get-tuple-element.170), channel_id=1, source_target_pairs={{16,0},{32,16},{48,32},{64,48},{80,64},{96,80},{112,96},{128,112},... | collective-permute-start | bytes 1105928 | tf_op jit(solution)/shard_map/ppermute | solution.py:25
  10.9 6.6 %collective-permute-start = (bf16[2,1440,64]{1,2,0:T(8,128)(2,1)S(1)}, bf16[2,1440,64]{1,2,0:T(8,128)(2,1)}, u32[]{:S(2)}, u32[]{:S(2)}) collective-permute-start(bf16[2,1440,64]{1,2,0:T(8,128)(2,1)S(1)} %get-tuple-element.169), channel_id=1, source_target_pairs={{0,16},{16,32},{32,48},{48,64},{64,80},{80,96},{96,112},{112,128},... | collective-permute-start | bytes 1105928 | tf_op jit(solution)/shard_map/ppermute | solution.py:23
  13.7 2.1 copy-start.14
  13.7 2.1 copy-start.15
  19.6 1.6 copy-start.1
  144.1 2.2 copy-start.5
  144.1 2.2 copy-start.12
  146.3 1.4 copy-start.6
  147.6 1.4 copy-start.7
  149.0 1.4 copy-start.8
  150.4 1.4 copy-start.9
  151.8 1.4 copy-start.10
  153.1 1.4 copy-start.11
  154.5 1.1 copy-start.3
  154.5 1.6 copy-start.4
  195.3 23.6 %all-to-all-start.1 = ((bf16[4,2,46080]{2,1,0:T(2,128)(2,1)}), bf16[4,2,46080]{2,1,0:T(2,128)(2,1)S(1)}, u32[]{:S(2)}, u32[]{:S(2)}) async-start(bf16[4,2,46080]{2,1,0:T(2,128)(2,1)} %reshape.556), calls=%async_computation.1 | async-start | bytes 1474560 | tf_op jit(solution)/shard_map/all_to_all | solution.py:106
  223.9 46.7 %copy-start.13 = (bf16[3,384,128]{2,1,0:T(8,128)(2,1)S(1)}, bf16[3,384,128]{2,1,0:T(8,128)(2,1)}, u32[]{:S(2)}) copy-start(bf16[3,384,128]{2,1,0:T(8,128)(2,1)} %param.17) | copy-start | bytes 884740
  256.8 13.7 %all-to-all-start.3 = ((bf16[128,12,128]{2,0,1:T(8,128)(2,1)}), bf16[128,12,128]{2,0,1:T(8,128)(2,1)S(1)}, u32[]{:S(2)}, u32[]{:S(2)}) async-start(bf16[128,12,128]{2,0,1:T(8,128)(2,1)} %bitcast.45), calls=%async_computation.3 | async-start | bytes 786432 | tf_op jit(solution)/shard_map/all_to_all | solution.py:109
where the time goes:
time: 277 us; the launch traced here: 273 us
  local copies, waits for them, and re-layouts  157 us (57%)
  blocking collectives  54.5 us (20%)
  starting transfers between devices  19.1 us (7%)
  other arithmetic  18.3 us (7%)
  matrix products  13.8 us (5%)
  waiting for transfers between devices  10.1 us (4%)
    gather x108, local copies, waits for them, and re-layouts  97.1 us
    all_to_all x1, blocking collectives, on_device(): lax.all_to_all(spectrum, 'lat', split_axis=1, concat_axis=0, tiled=True)  31.9 us
    unnamed x51, local copies, waits for them, and re-layouts  23.8 us
    all_to_all x1, blocking collectives, on_device(): lax.all_to_all(mixed, 'chan', split_axis=0, concat_axis=2, tiled=True)  22.6 us
    concatenate x1, local copies, waits for them, and re-layouts, on_device(): jnp.concatenate([padded[:, lon_count - DLON:], padded, padded[:, :DLON]],...  13.7 us
    neg x1, other arithmetic, fourier_table(): -jnp.sin(angle)  9.19 us
    all_to_all x1, waiting for transfers between devices, on_device(): lax.all_to_all(lax.all_to_all(spectrum, 'lat', split_axis=1, concat_axis=...  9.02 us
    ppermute x1, starting transfers between devices, with_halo(): lax.ppermute(head, axis, [((i + 1) % count, i) for i in range(ends)])  8.9 us
  transfers between devices with their start and end apart: 4, of which 2 were waited for; matrix products, arithmetic and copies ran while one was open for 9% of the time, Pallas kernels for 0%

commit v1 on v0

v1 whole, which is shorter than its diff:
```python
import functools
import math

import jax
import jax.numpy as jnp
import ml_dtypes
import numpy as np
from jax import lax
from jax.experimental import pallas as pl
from jax.experimental.pallas import tpu as pltpu
from jax.sharding import PartitionSpec as P

G = 64
NB = 6
S = 9
HALO = 2
DLON = 4
LANES = 128
CHUNK = 384
PAD = 16


def fourier_rows(lon_count, lon_pad, mode_count, mode_dev):
    lon = np.arange(lon_count, dtype=np.int64)
    mode = np.arange(mode_count, dtype=np.int64)
    phase = (lon[:, None] * mode[None, :]) % lon_count
    angle = phase.astype(np.float32) * np.float32(2.0 * math.pi / lon_count)
    scale = np.float32(math.sqrt(2.0 / lon_count))
    table = np.zeros((mode_count // mode_dev, PAD // 2, lon_pad), np.float32)
    pair = np.stack([np.cos(angle), -np.sin(angle)], axis=-1) * scale
    pair = pair.reshape(lon_count, mode_count // mode_dev, 2 * mode_dev)
    table[:, : 2 * mode_dev, :lon_count] = np.transpose(pair, (1, 2, 0))
    return table.reshape(-1, lon_pad).astype(ml_dtypes.bfloat16)


def spread(block, ext, row, lon_count):
    chans = block.shape[0]
    tiles = -(-lon_count // LANES)
    last = lon_count - (tiles - 1) * LANES
    lane = lax.broadcasted_iota(jnp.int32, (chans, LANES), 1)
    pieces = [block[:, t * LANES : min((t + 1) * LANES, lon_count)].astype(jnp.float32) for t in range(tiles)]
    if last < LANES:
        pieces[-1] = jnp.concatenate([pieces[-1], jnp.zeros((chans, LANES - last), jnp.float32)], axis=1)
    turned = [pltpu.roll(p, DLON, 1) for p in pieces]
    before = pltpu.roll(pieces[-1], (LANES - last + DLON) % LANES, 1)
    after = pltpu.roll(pieces[0], last + DLON, 1)
    for t in range(tiles):
        left = before if t == 0 else turned[t - 1]
        value = jnp.where(lane < DLON, left, turned[t])
        if t == tiles - 1:
            value = jnp.where(lane < last + DLON, value, jnp.where(lane < last + 2 * DLON, after, 0.0))
        ext[row, :, t * LANES : (t + 1) * LANES] = value.astype(ext.dtype)
    ext[row, :, tiles * LANES :] = jnp.zeros((chans, ext.shape[2] - tiles * LANES), ext.dtype)


def make_filters(row, basis, value, twice, filters):
    lane = lax.broadcasted_iota(jnp.int32, (G, LANES), 1)
    for pair in range(0, S, 2):
        first = twice[basis[row, pair]].astype(jnp.float32) * value[row, pair]
        if pair + 1 < S:
            second = twice[basis[row, pair + 1]].astype(jnp.float32) * value[row, pair + 1]
            first = jnp.where(lane < G, first, second)
            filters[row, :, pair * G : (pair + 2) * G] = first.astype(filters.dtype)
        else:
            filters[row, :, pair * G : (pair + 1) * G] = first[:, :G].astype(filters.dtype)


def disco_chunk(row, start, shift_lat, shift_lon, ext, filters, columns):
    lane = lax.broadcasted_iota(jnp.int32, (G, LANES), 1)
    for tap in range(S):
        source = row + HALO + shift_lat[row, tap]
        turn = DLON + shift_lon[row, tap]
        held = ext[source, :, pl.ds(start, CHUNK + LANES)]
        turned = [
            pltpu.roll(held[:, t * LANES : (t + 1) * LANES], LANES - turn, 1)
            for t in range(CHUNK // LANES + 1)
        ]
        for t in range(CHUNK // LANES):
            columns[tap * G : (tap + 1) * G, t * LANES : (t + 1) * LANES] = jnp.where(
                lane < LANES - turn, turned[t], turned[t + 1]
            ).astype(columns.dtype)
    return jnp.dot(filters[row], columns[...], preferred_element_type=jnp.float32)


def disco_kernel(shift_lat, shift_lon, basis, value, fields, low, high, twice, out, ext, filters, columns):
    lat_dev, chans, lon_count = fields.shape
    chunks = out.shape[1]
    for r in range(HALO):
        spread(low[r], ext, r, lon_count)
        spread(high[r], ext, HALO + lat_dev + r, lon_count)
    for r in range(lat_dev):
        spread(fields[r], ext, HALO + r, lon_count)
        make_filters(r, basis, value, twice, filters)
    for c in range(chunks):
        start = c * CHUNK
        width = min(CHUNK, lon_count - start)
        for r in range(lat_dev):
            total = disco_chunk(r, start, shift_lat, shift_lon, ext, filters, columns)
            own = fields[r, :, start : start + width].astype(jnp.float32)
            out[r, c, :, :width] = (own + total[:, :width]).astype(out.dtype)
            if width < CHUNK:
                out[r, c, :, width:] = jnp.zeros((chans, CHUNK - width), out.dtype)


def mlp_chunk(mixed, up, down):
    values = mixed.astype(jnp.float32)
    center = values - jnp.mean(values, axis=0, keepdims=True)
    variance = jnp.mean(center * center, axis=0, keepdims=True)
    normed = (center * lax.rsqrt(variance + 1e-05)).astype(jnp.bfloat16)
    lifted = jnp.dot(up, normed, preferred_element_type=jnp.float32)
    inner = math.sqrt(2.0 / math.pi) * (lifted + 0.044715 * (lifted * lifted * lifted))
    active = (0.5 * lifted * (1.0 + jnp.tanh(inner))).astype(jnp.bfloat16)
    lowered = jnp.dot(down, active, preferred_element_type=jnp.float32)
    return (values + lowered).astype(jnp.bfloat16)


def store_spectrum(spectrum, out):
    half = PAD // 2
    for h in range(2):
        piece = spectrum[:, h * LANES : (h + 1) * LANES].astype(jnp.bfloat16)
        out[:, h * half : (h + 1) * half, :] = piece.reshape(out.shape[0], half, LANES)


def mlp_kernel(mixed, w_up, w_down, table, out):
    peers, chunks, chans, _ = mixed.shape
    up = w_up[...].T
    down = w_down[...].T
    total = None
    for c in range(chunks):
        block = jnp.concatenate([mixed[p, c] for p in range(peers)], axis=0)
        done = mlp_chunk(block, up, down)
        part = lax.dot_general(
            table[:, c * CHUNK : (c + 1) * CHUNK], done, (((1,), (1,)), ((), ())),
            preferred_element_type=jnp.float32,
        )
        total = part if total is None else total + part
    store_spectrum(total, out)


def legendre_kernel(spectrum, legendre, out, wide):
    lats = spectrum.shape[0]
    mode_dev, degrees, _ = legendre.shape
    me = lax.axis_index("lat") * lax.axis_size("chan") + lax.axis_index("chan")
    wide[...] = spectrum[...].astype(jnp.float32).reshape(lats * PAD, LANES)
    degree = lax.broadcasted_iota(jnp.int32, (degrees, lats), 0)
    for m in range(mode_dev):
        kept = jnp.where(degree >= me * mode_dev + m, legendre[m].astype(jnp.float32), 0.0).astype(jnp.bfloat16)
        rows = [h * (PAD // 2) + 2 * m + r for r in range(2) for h in range(2)]
        right = jnp.concatenate(
            [wide[pl.ds(j, lats, stride=PAD), :].astype(jnp.bfloat16) for j in rows], axis=1
        )
        out[m] = jnp.dot(kept, right, preferred_element_type=jnp.float32).astype(out.dtype)


def on_device(
    fields, disco_weight, support_lat, support_lon, support_basis, support_value, w_up, w_down, legendre
):
    lat_dev, lon_count, chans = fields.shape
    num_lat = lax.axis_size("lat")
    num_chan = lax.axis_size("chan")
    mode_dev, degrees, _ = legendre.shape
    devices = num_lat * num_chan
    chunks = -(-lon_count // CHUNK)
    smem = pl.BlockSpec(memory_space=pltpu.SMEM)
    vmem = pl.BlockSpec(memory_space=pltpu.VMEM)
    params = pltpu.CompilerParams(vmem_limit_bytes=56 << 20)
    turned = jnp.swapaxes(fields, 1, 2)
    twice = jnp.concatenate([disco_weight, disco_weight], axis=2)
    ends = num_lat - 1
    low = lax.ppermute(turned[lat_dev - HALO :], "lat", [(i, i + 1) for i in range(ends)])
    high = lax.ppermute(turned[:HALO], "lat", [(i + 1, i) for i in range(ends)])
    ext_lanes = chunks * CHUNK + LANES
    mixed = pl.pallas_call(
        disco_kernel,
        out_shape=jax.ShapeDtypeStruct((lat_dev, chunks, chans, CHUNK), jnp.bfloat16),
        in_specs=[smem] * 4 + [vmem] * 4,
        out_specs=vmem,
        scratch_shapes=[
            pltpu.VMEM((lat_dev + 2 * HALO, chans, ext_lanes), jnp.float32),
            pltpu.VMEM((lat_dev, G, S * G), jnp.bfloat16),
            pltpu.VMEM((S * G, CHUNK), jnp.bfloat16),
        ],
        compiler_params=params,
        name="disco",
    )(support_lat, support_lon, support_basis, support_value, turned, low, high, twice)
    mixed = lax.all_to_all(mixed, "chan", split_axis=0, concat_axis=0, tiled=True)
    table = jnp.asarray(fourier_rows(lon_count, chunks * CHUNK, mode_dev * devices, mode_dev))
    spectrum = pl.pallas_call(
        mlp_kernel,
        out_shape=jax.ShapeDtypeStruct((devices, PAD, LANES), jnp.bfloat16),
        in_specs=[vmem] * 4,
        out_specs=vmem,
        compiler_params=params,
        name="mlp",
    )(mixed, w_up, w_down, table)
    spectrum = lax.all_to_all(spectrum, ("lat", "chan"), split_axis=0, concat_axis=0, tiled=True)
    return pl.pallas_call(
        legendre_kernel,
        out_shape=jax.ShapeDtypeStruct((mode_dev, degrees, 4 * LANES), jnp.bfloat16),
        in_specs=[vmem] * 2,
        out_specs=vmem,
        scratch_shapes=[pltpu.VMEM((devices * PAD, LANES), jnp.float32)],
        compiler_params=params,
        name="legendre",
    )(spectrum, legendre)


def solution(mesh):
    in_specs = (
        P(("tm", "lat"), None, "chan"),
        P(None, "chan", None),
        P("lat", None),
        P("lat", None),
        P("lat", None),
        P("lat", None),
        P(),
        P(),
        P(("lat", "chan"), None, None),
    )
    out_specs = P(("tm", "lat", "chan"), None, None)
    return jax.shard_map(
        on_device, mesh=mesh, in_specs=in_specs, out_specs=out_specs, check_vma=False
    )
```

time: 277 us -> 91.4 us (0.33); the launches traced: 273 us -> 91.1 us
  local copies, waits for them, and re-layouts: 157 us -> 1.91 us
  other arithmetic: 18.3 us -> 1.7 us
  Pallas kernels: 0 us -> 16 us
  matrix products: 13.8 us -> 0 us
  starting transfers between devices: 19.1 us -> 10.7 us
  waiting for transfers between devices: 10.1 us -> 3 us
  blocking collectives: 54.5 us -> 57.8 us
    gather x108 -> x0, local copies, waits for them, and re-layouts: 97.1 us -> none
    unnamed x51 -> x4, local copies, waits for them, and re-layouts: 23.8 us -> 0.75 us
    pallas_call x0 -> x3, Pallas kernels: none -> 16 us  [the longest x1 6.9 us: on_device(): pl.pallas_call(mlp_kernel, out_shape=jax.ShapeDtypeStruct((devices, PAD,...]
    convert_element_type x8 -> x0, local copies, waits for them, and re-layouts: 15.1 us -> none  [the longest x2 8.81 us: fourier_table(): return paired.reshape(lon_count, 2 * mode_count).astype(jnp.bfloat16)]
    concatenate x1 -> x0, local copies, waits for them, and re-layouts: 13.7 us -> none  [on_device(): jnp.concatenate([padded[:, lon_count - DLON:], padded, padded[:, :DLON]],...]
    dot_general x11 -> x0, matrix products: 10.8 us -> none  [the longest x9 7.21 us: on_device(): jnp.einsum('anhi,ahoi->anho', slab, filters[:, position], preferred_eleme...]
    neg x1 -> x0, other arithmetic: 9.19 us -> none  [fourier_table(): -jnp.sin(angle)]
    all_to_all x2 -> x0, waiting for transfers between devices: 9.03 us -> none  [the longest x1 9.02 us: on_device(): lax.all_to_all(lax.all_to_all(spectrum, 'lat', split_axis=1, concat_axis=...]
  transfers between devices with their start and end apart: 4 -> 2, of which waited for: 2 -> 1; matrix products, arithmetic and copies ran while one was open for 9% -> 2% of each run, Pallas kernels for 0% -> 0%
where the time goes in v1:
time: 91.4 us; the launch traced here: 91.1 us
  blocking collectives  57.8 us (63%)
  Pallas kernels  16 us (18%)
  starting transfers between devices  10.7 us (12%)
  waiting for transfers between devices  3 us (3%)
  local copies, waits for them, and re-layouts  1.91 us (2%)
  other arithmetic  1.7 us (2%)
    all_to_all x1, blocking collectives, on_device(): lax.all_to_all(spectrum, ('lat', 'chan'), split_axis=0, concat_axis=0, ti...  34.4 us
    all_to_all x1, blocking collectives, on_device(): lax.all_to_all(mixed, 'chan', split_axis=0, concat_axis=0, tiled=True)  23.4 us
    ppermute x1, starting transfers between devices, on_device(): high = lax.ppermute(turned[:HALO], 'lat', [(i + 1, i) for i in range(ends)])  8.79 us
    pallas_call x1, Pallas kernels, on_device(): pl.pallas_call(mlp_kernel, out_shape=jax.ShapeDtypeStruct((devices, PAD,...  6.9 us
    pallas_call x1, Pallas kernels, on_device(): pl.pallas_call(disco_kernel, out_shape=jax.ShapeDtypeStruct((lat_dev, chu...  6.35 us
    ppermute x1, waiting for transfers between devices, on_device(): lax.ppermute(turned[lat_dev - HALO:], 'lat', [(i, i + 1) for i in range(e...  2.99 us
    pallas_call x1, Pallas kernels, on_device(): pl.pallas_call(legendre_kernel, out_shape=jax.ShapeDtypeStruct((mode_dev,...  2.71 us
    ppermute x1, starting transfers between devices, on_device(): lax.ppermute(turned[lat_dev - HALO:], 'lat', [(i, i + 1) for i in range(e...  1.92 us
  transfers between devices with their start and end apart: 2, of which 1 were waited for; matrix products, arithmetic and copies ran while one was open for 2% of the time, Pallas kernels for 0%

profile of v1, /device:TPU:1, one launch (start us, length us, event | category | flops | bytes accessed | tf_op | source)
XLA Modules:
  0.0 91.1 jit_solution(12850892351214659638)
XLA Ops:
  0.0 1.2 %fusion = (bf16[2,64,1440]{2,1,0:T(8,128)(2,1)S(1)}, bf16[2,64,1440]{2,1,0:T(8,128)(2,1)S(1)}) fusion(bf16[4,64,1440]{2,1,0:T(8,128)(2,1)} %bitcast.1), kind=kLoop, calls=%fused_computation.1 | loop fusion | bytes 1474560 | tf_op jit(solution)/shard_map/slice | solution.py:171
  1.2 8.8 %collective-permute-start.1 = (bf16[2,64,1440]{2,1,0:T(8,128)(2,1)S(1)}, bf16[2,64,1440]{2,1,0:T(8,128)(2,1)S(1)}, u32[]{:S(2)}, u32[]{:S(2)}) collective-permute-start(bf16[2,64,1440]{2,1,0:T(8,128)(2,1)S(1)} %get-tuple-element.5), channel_id=1, source_target_pairs={{16,0},{32,16},{48,32},{64,48},{80,64},{96,80},{112,96},{128,112},... | collective-permute-start | bytes 1105928 | tf_op jit(solution)/shard_map/ppermute | solution.py:171
  10.0 1.9 %collective-permute-start = (bf16[2,64,1440]{2,1,0:T(8,128)(2,1)S(1)}, bf16[2,64,1440]{2,1,0:T(8,128)(2,1)S(1)}, u32[]{:S(2)}, u32[]{:S(2)}) collective-permute-start(bf16[2,64,1440]{2,1,0:T(8,128)(2,1)S(1)} %get-tuple-element.6), channel_id=1, source_target_pairs={{0,16},{16,32},{32,48},{48,64},{64,80},{80,96},{96,112},{112,128},... | collective-permute-start | bytes 1105928 | tf_op jit(solution)/shard_map/ppermute | solution.py:170
  11.9 1.7 %pad_maximum_fusion.twice = bf16[6,64,128]{2,1,0:T(8,128)(2,1)} fusion(bf16[6,64,64]{2,1,0:T(8,128)(2,1)} %param.11), kind=kLoop, calls=%fused_computation | loop fusion | flops 196608 | bytes 147456 | tf_op jit(solution)/shard_map/concatenate | solution.py:168
  13.6 0.0 collective-permute-done.1.high
  13.6 0.0 copy-start
  13.6 3.0 %collective-permute-done.low = bf16[2,64,1440]{2,1,0:T(8,128)(2,1)S(1)} collective-permute-done((bf16[2,64,1440]{2,1,0:T(8,128)(2,1)S(1)}, bf16[2,64,1440]{2,1,0:T(8,128)(2,1)S(1)}, u32[]{:S(2)}, u32[]{:S(2)}) %collective-permute-start) | collective-permute-done | bytes 368672 | tf_op jit(solution)/shard_map/ppermute | solution.py:170
  16.6 0.0 copy-done
  16.6 0.0 copy-start.1
  16.6 0.7 copy-done.1
  17.3 6.3 %disco.1 = bf16[4,4,64,384]{3,2,1,0:T(8,128)(2,1)} custom-call(s32[4,9]{1,0:T(4,128)} %shift_lat.1, s32[4,9]{1,0:T(4,128)} %shift_lon.1, s32[4,9]{1,0:T(4,128)} %basis.1, f32[4,9]{1,0:T(4,128)} %value.1, bf16[4,64,1440]{2,1,0:T(8,128)(2,1)} %bitcast.2, bf16[2,64,1440]{2,1,0:T(8,128)(2,1)} %copy-done.1, bf16[2,64,1440]{2,1,0:T(8,128)(2,1)} %copy-done, ...), custom_call_target="tpu_custom_call" | custom-call | tf_op jit(solution)/shard_map/disco/pallas_call | solution.py:173
  23.7 23.4 %all_to_all.10.mixed = bf16[4,4,64,384]{3,2,1,0:T(8,128)(2,1)} all-to-all(bf16[4,4,64,384]{3,2,1,0:T(8,128)(2,1)} %disco.1), channel_id=1, replica_groups=mesh['lat'=32,'chan'=4,'tm'=4] {'chan'}, dimensions={0} | all-to-all | bytes 1572864 | tf_op jit(solution)/shard_map/all_to_all | solution.py:186
  47.1 6.9 %mlp.1 = bf16[128,16,128]{2,1,0:T(8,128)(2,1)} custom-call(bf16[4,4,64,384]{3,2,1,0:T(8,128)(2,1)} %all_to_all.10.mixed, bf16[256,512]{1,0:T(8,128)(2,1)} %w_up.1, bf16[512,256]{1,0:T(8,128)(2,1)} %w_down.1, bf16[1024,1536]{1,0:T(8,128)(2,1)} %constant.2.clone.table), custom_call_target="tpu_custom_call" | custom-call | tf_op jit(solution)/shard_map/mlp/pallas_call | solution.py:188
  54.0 34.4 %all_to_all.11.spectrum = bf16[128,16,128]{2,1,0:T(8,128)(2,1)} all-to-all(bf16[128,16,128]{2,1,0:T(8,128)(2,1)} %mlp.1), channel_id=1, replica_groups=mesh['lat'=32,'chan'=4,'tm'=4] {'lat','chan'}, dimensions={0} | all-to-all | bytes 1048576 | tf_op jit(solution)/shard_map/all_to_all | solution.py:196
  88.4 2.7 %legendre.2 = bf16[3,384,512]{2,1,0:T(8,128)(2,1)} custom-call(bf16[128,16,128]{2,1,0:T(8,128)(2,1)} %all_to_all.11.spectrum, bf16[3,384,128]{2,1,0:T(8,128)(2,1)} %legendre.3), custom_call_target="tpu_custom_call" | custom-call | tf_op jit(solution)/shard_map/legendre/pallas_call | solution.py:197
Async XLA Ops:
  1.2 12.4 %collective-permute-start.1 = (bf16[2,64,1440]{2,1,0:T(8,128)(2,1)S(1)}, bf16[2,64,1440]{2,1,0:T(8,128)(2,1)S(1)}, u32[]{:S(2)}, u32[]{:S(2)}) collective-permute-start(bf16[2,64,1440]{2,1,0:T(8,128)(2,1)S(1)} %get-tuple-element.5), channel_id=1, source_target_pairs={{16,0},{32,16},{48,32},{64,48},{80,64},{96,80},{112,96},{128,112},... | collective-permute-start | bytes 1105928 | tf_op jit(solution)/shard_map/ppermute | solution.py:171
  10.0 6.6 %collective-permute-start = (bf16[2,64,1440]{2,1,0:T(8,128)(2,1)S(1)}, bf16[2,64,1440]{2,1,0:T(8,128)(2,1)S(1)}, u32[]{:S(2)}, u32[]{:S(2)}) collective-permute-start(bf16[2,64,1440]{2,1,0:T(8,128)(2,1)S(1)} %get-tuple-element.6), channel_id=1, source_target_pairs={{0,16},{16,32},{32,48},{48,64},{64,80},{80,96},{96,112},{112,128},... | collective-permute-start | bytes 1105928 | tf_op jit(solution)/shard_map/ppermute | solution.py:170
  13.6 3.0 %copy-start = (bf16[2,64,1440]{2,1,0:T(8,128)(2,1)}, bf16[2,64,1440]{2,1,0:T(8,128)(2,1)S(1)}, u32[]{:S(2)}) copy-start(bf16[2,64,1440]{2,1,0:T(8,128)(2,1)S(1)} %collective-permute-done.1.high) | copy-start | bytes 1105924
  16.6 0.7 copy-start.1

commit v2 on v1

v2 whole, which is shorter than its diff:
```python
import functools
import math

import jax
import jax.numpy as jnp
import ml_dtypes
import numpy as np
from jax import lax
from jax.experimental import pallas as pl
from jax.experimental.pallas import tpu as pltpu
from jax.sharding import PartitionSpec as P

G = 64
NB = 6
S = 9
HALO = 2
DLON = 4
LANES = 128
CHUNK = 384
PAD = 16
MESH = pl.DeviceIdType.MESH


def fourier_rows(lon_count, lon_pad, mode_count, mode_dev):
    lon = np.arange(lon_count, dtype=np.int64)
    mode = np.arange(mode_count, dtype=np.int64)
    phase = (lon[:, None] * mode[None, :]) % lon_count
    angle = phase.astype(np.float32) * np.float32(2.0 * math.pi / lon_count)
    scale = np.float32(math.sqrt(2.0 / lon_count))
    table = np.zeros((mode_count // mode_dev, PAD // 2, lon_pad), np.float32)
    pair = np.stack([np.cos(angle), -np.sin(angle)], axis=-1) * scale
    pair = pair.reshape(lon_count, mode_count // mode_dev, 2 * mode_dev)
    table[:, : 2 * mode_dev, :lon_count] = np.transpose(pair, (1, 2, 0))
    return table.reshape(-1, lon_pad).astype(ml_dtypes.bfloat16)


def spread(block, ext, row, lon_count):
    chans = block.shape[0]
    tiles = -(-lon_count // LANES)
    last = lon_count - (tiles - 1) * LANES
    lane = lax.broadcasted_iota(jnp.int32, (chans, LANES), 1)
    pieces = [block[:, t * LANES : min((t + 1) * LANES, lon_count)].astype(jnp.float32) for t in range(tiles)]
    if last < LANES:
        pieces[-1] = jnp.concatenate([pieces[-1], jnp.zeros((chans, LANES - last), jnp.float32)], axis=1)
    turned = [pltpu.roll(p, DLON, 1) for p in pieces]
    before = pltpu.roll(pieces[-1], (LANES - last + DLON) % LANES, 1)
    after = pltpu.roll(pieces[0], last + DLON, 1)
    for t in range(tiles):
        left = before if t == 0 else turned[t - 1]
        value = jnp.where(lane < DLON, left, turned[t])
        if t == tiles - 1:
            value = jnp.where(lane < last + DLON, value, jnp.where(lane < last + 2 * DLON, after, 0.0))
        ext[row, :, t * LANES : (t + 1) * LANES] = value.astype(ext.dtype)
    ext[row, :, tiles * LANES :] = jnp.zeros((chans, ext.shape[2] - tiles * LANES), ext.dtype)


def make_filters(row, basis, value, weight, filters):
    for pair in range(0, S, 2):
        parts = [
            weight[basis[row, tap]].astype(jnp.float32) * value[row, tap]
            for tap in range(pair, min(pair + 2, S))
        ]
        joined = parts[0] if len(parts) == 1 else jnp.concatenate(parts, axis=1)
        filters[row, :, pair * G : (pair + len(parts)) * G] = joined.astype(filters.dtype)


def disco_chunk(row, start, shift_lat, shift_lon, ext, filters, columns):
    lane = lax.broadcasted_iota(jnp.int32, (G, LANES), 1)
    for tap in range(S):
        source = row + HALO + shift_lat[row, tap]
        turn = DLON + shift_lon[row, tap]
        held = ext[source, :, pl.ds(start, CHUNK + LANES)]
        turned = [
            pltpu.roll(held[:, t * LANES : (t + 1) * LANES], LANES - turn, 1)
            for t in range(CHUNK // LANES + 1)
        ]
        for t in range(CHUNK // LANES):
            columns[tap * G : (tap + 1) * G, t * LANES : (t + 1) * LANES] = jnp.where(
                lane < LANES - turn, turned[t], turned[t + 1]
            ).astype(columns.dtype)
    return jnp.dot(filters[row], columns[...], preferred_element_type=jnp.float32)


def block_kernel(
    num_lat,
    num_chan,
    shift_lat,
    shift_lon,
    basis,
    value,
    fields,
    weight,
    w_up,
    w_down,
    table_hbm,
    legendre_hbm,
    out,
    own,
    halo,
    ext,
    filters,
    columns,
    mixed,
    gathered,
    up,
    down,
    table,
    legendre,
    total,
    sent,
    taken,
    wide,
    load_sem,
    halo_send,
    halo_recv,
    mix_send,
    mix_recv,
    spec_send,
    spec_recv,
):
    lat_dev, chans, lon_count = fields.shape
    chunks = mixed.shape[1]
    mode_dev, degrees, lats = legendre.shape
    devices = num_lat * num_chan
    half = lat_dev // 2
    band = lax.axis_index("lat")
    mine = lax.axis_index("chan")
    me = band * num_chan + mine
    core = lax.rem(band, 2)

    def device(index):
        return {"lat": lax.div(index, num_chan), "chan": lax.rem(index, num_chan)}

    loads = [
        pltpu.make_async_copy(table_hbm, table, load_sem.at[0]),
        pltpu.make_async_copy(legendre_hbm, legendre, load_sem.at[1]),
    ]
    for load in loads:
        load.start()
    barrier = pltpu.get_barrier_semaphore()

    def greet(step, carry):
        pl.semaphore_signal(
            barrier, inc=1, device_id=device(lax.rem(me + step, devices)), device_id_type=MESH
        )
        return carry

    lax.fori_loop(1, devices, greet, 0)
    pl.semaphore_wait(barrier, devices - 1)

    upward = pltpu.make_async_remote_copy(
        src_ref=fields.at[pl.ds(lat_dev - HALO, HALO)],
        dst_ref=halo.at[0],
        send_sem=halo_send.at[0],
        recv_sem=halo_recv.at[0],
        device_id={"lat": band + 1},
        device_id_type=MESH,
    )
    downward = pltpu.make_async_remote_copy(
        src_ref=fields.at[pl.ds(0, HALO)],
        dst_ref=halo.at[1],
        send_sem=halo_send.at[1],
        recv_sem=halo_recv.at[1],
        device_id={"lat": band - 1},
        device_id_type=MESH,
    )

    @pl.when(band < num_lat - 1)
    def _():
        upward.start()

    @pl.when(band > 0)
    def _():
        downward.start()

    for row in range(lat_dev):
        spread(fields[row], ext, HALO + row, lon_count)
        make_filters(row, basis, value, weight, filters)
    up[...] = w_up[...].T
    down[...] = w_down[...].T

    def disco_row(row, c):
        start = pl.multiple_of(c * CHUNK, LANES)
        acc = disco_chunk(row, start, shift_lat, shift_lon, ext, filters, columns)
        here = ext_own[row, :, pl.ds(start, CHUNK)].astype(jnp.float32)
        result = (here + acc).astype(mixed.dtype)

        @pl.when(row == mine)
        def _():
            gathered[c, mine] = result

        @pl.when(row != mine)
        def _():
            mixed[row, c] = result
            pltpu.make_async_remote_copy(
                src_ref=mixed.at[row, c],
                dst_ref=gathered.at[c, mine],
                send_sem=mix_send,
                recv_sem=mix_recv.at[c],
                device_id={"chan": row},
                device_id_type=MESH,
            ).start()

    ext_own = own
    for row in range(lat_dev):
        own[row, :, :lon_count] = fields[row]
        own[row, :, lon_count:] = jnp.zeros((chans, own.shape[2] - lon_count), own.dtype)
    for turn in range(2):
        side = 1 - core if turn == 0 else core
        present = jnp.where(side == 0, band > 0, band < num_lat - 1)

        @pl.when(present)
        def _():
            pltpu.make_async_copy(halo.at[side], halo.at[side], halo_recv.at[side]).wait()

        @pl.when(jnp.logical_not(present))
        def _():
            halo[side] = jnp.zeros(halo.shape[1:], halo.dtype)

        for r in range(HALO):
            spread(halo[side, r], ext, side * (HALO + lat_dev) + r, lon_count)

        def steps(step, carry):
            disco_row(side * half + lax.rem(step, half), lax.div(step, half))
            return carry

        lax.fori_loop(0, half * chunks, steps, 0)

    loads[0].wait()

    def mlp_part(c):
        pltpu.make_async_copy(
            gathered.at[c, pl.ds(0, num_chan - 1)],
            gathered.at[c, pl.ds(0, num_chan - 1)],
            mix_recv.at[c],
        ).wait()
        block = gathered[c].reshape(num_chan * chans, CHUNK)
        done = mlp_chunk(block, up[...], down[...])
        return lax.dot_general(
            table[:, pl.ds(pl.multiple_of(c * CHUNK, LANES), CHUNK)],
            done,
            (((1,), (1,)), ((), ())),
            preferred_element_type=jnp.float32,
        )

    total[...] = mlp_part(0)

    def mlp_step(c, carry):
        total[...] += mlp_part(c)
        return carry

    lax.fori_loop(1, chunks, mlp_step, 0)
    rows = PAD // 2
    for h in range(2):
        piece = total[:, h * LANES : (h + 1) * LANES].astype(jnp.bfloat16)
        sent[:, h * rows : (h + 1) * rows, :] = piece.reshape(devices, rows, LANES)

    def hand_out(step, carry):
        to = lax.rem(me + step, devices)
        pltpu.make_async_remote_copy(
            src_ref=sent.at[to],
            dst_ref=taken.at[me],
            send_sem=spec_send,
            recv_sem=spec_recv,
            device_id=device(to),
            device_id_type=MESH,
        ).start()
        return carry

    lax.fori_loop(1, devices, hand_out, 0)
    taken[me] = sent[me]
    loads[1].wait()
    degree = lax.broadcasted_iota(jnp.int32, (degrees, lats), 0)
    for m in range(mode_dev):
        kept = jnp.where(degree >= me * mode_dev + m, legendre[m].astype(jnp.float32), 0.0)
        legendre[m] = kept.astype(jnp.bfloat16)
    pltpu.make_async_copy(
        taken.at[pl.ds(0, devices - 1)], taken.at[pl.ds(0, devices - 1)], spec_recv
    ).wait()
    wide[...] = taken[...].astype(jnp.float32).reshape(devices * PAD, LANES)
    for m in range(mode_dev):
        picks = [h * rows + 2 * m + r for r in range(2) for h in range(2)]
        right = jnp.concatenate(
            [wide[pl.ds(j, devices, stride=PAD), :].astype(jnp.bfloat16) for j in picks], axis=1
        )
        out[m] = jnp.dot(legendre[m], right, preferred_element_type=jnp.float32).astype(out.dtype)
    pltpu.make_async_copy(mixed.at[pl.ds(0, lat_dev - 1)], mixed.at[pl.ds(0, lat_dev - 1)], mix_send).wait()
    pltpu.make_async_copy(sent.at[pl.ds(0, devices - 1)], sent.at[pl.ds(0, devices - 1)], spec_send).wait()

    @pl.when(band < num_lat - 1)
    def _():
        upward.wait_send()

    @pl.when(band > 0)
    def _():
        downward.wait_send()


def mlp_chunk(mixed, up, down):
    values = mixed.astype(jnp.float32)
    center = values - jnp.mean(values, axis=0, keepdims=True)
    variance = jnp.mean(center * center, axis=0, keepdims=True)
    normed = (center * lax.rsqrt(variance + 1e-05)).astype(jnp.bfloat16)
    lifted = jnp.dot(up, normed, preferred_element_type=jnp.float32)
    inner = math.sqrt(2.0 / math.pi) * (lifted + 0.044715 * (lifted * lifted * lifted))
    active = (0.5 * lifted * (1.0 + jnp.tanh(inner))).astype(jnp.bfloat16)
    lowered = jnp.dot(down, active, preferred_element_type=jnp.float32)
    return (values + lowered).astype(jnp.bfloat16)


def on_device(
    fields, disco_weight, support_lat, support_lon, support_basis, support_value, w_up, w_down, legendre
):
    lat_dev, lon_count, chans = fields.shape
    num_lat = lax.axis_size("lat")
    num_chan = lax.axis_size("chan")
    mode_dev, degrees, lats = legendre.shape
    devices = num_lat * num_chan
    chunks = -(-lon_count // CHUNK)
    lon_pad = chunks * CHUNK
    hidden = w_up.shape[1]
    smem = pl.BlockSpec(memory_space=pltpu.SMEM)
    vmem = pl.BlockSpec(memory_space=pltpu.VMEM)
    hbm = pl.BlockSpec(memory_space=pl.ANY)
    bf16, f32 = jnp.bfloat16, jnp.float32
    dma = pltpu.SemaphoreType.DMA
    table = jnp.asarray(fourier_rows(lon_count, lon_pad, mode_dev * devices, mode_dev))
    return pl.pallas_call(
        functools.partial(block_kernel, num_lat, num_chan),
        out_shape=jax.ShapeDtypeStruct((mode_dev, degrees, 4 * LANES), bf16),
        in_specs=[smem] * 4 + [vmem] * 4 + [hbm] * 2,
        out_specs=vmem,
        scratch_shapes=[
            pltpu.VMEM((lat_dev, chans, lon_pad), bf16),
            pltpu.VMEM((2, HALO, chans, lon_count), bf16),
            pltpu.VMEM((lat_dev + 2 * HALO, chans, lon_pad + LANES), f32),
            pltpu.VMEM((lat_dev, G, S * G), bf16),
            pltpu.VMEM((S * G, CHUNK), bf16),
            pltpu.VMEM((lat_dev, chunks, chans, CHUNK), bf16),
            pltpu.VMEM((chunks, num_chan, chans, CHUNK), bf16),
            pltpu.VMEM((hidden, num_chan * chans), bf16),
            pltpu.VMEM((num_chan * chans, hidden), bf16),
            pltpu.VMEM(table.shape, bf16),
            pltpu.VMEM(legendre.shape, bf16),
            pltpu.VMEM((devices * PAD // 2, num_chan * chans), f32),
            pltpu.VMEM((devices, PAD, LANES), bf16),
            pltpu.VMEM((devices, PAD, LANES), bf16),
            pltpu.VMEM((devices * PAD, LANES), f32),
            dma((2,)),
            dma((2,)),
            dma((2,)),
            dma,
            dma((chunks,)),
            dma,
            dma,
        ],
        compiler_params=pltpu.CompilerParams(
            collective_id=0, has_side_effects=True, vmem_limit_bytes=56 << 20
        ),
        name="block",
    )(
        support_lat,
        support_lon,
        support_basis,
        support_value,
        jnp.swapaxes(fields, 1, 2),
        disco_weight,
        w_up,
        w_down,
        table,
        legendre,
    )


def solution(mesh):
    in_specs = (
        P(("tm", "lat"), None, "chan"),
        P(None, "chan", None),
        P("lat", None),
        P("lat", None),
        P("lat", None),
        P("lat", None),
        P(),
        P(),
        P(("lat", "chan"), None, None),
    )
    out_specs = P(("tm", "lat", "chan"), None, None)
    return jax.shard_map(
        on_device, mesh=mesh, in_specs=in_specs, out_specs=out_specs, check_vma=False
    )
```

time: 91.4 us -> 66.4 us (0.73)
  blocking collectives: 57.8 us -> 0 us
  Pallas kernels: 16 us -> 63.8 us
  starting transfers between devices: 10.7 us -> 0 us
  waiting for transfers between devices: 3 us -> 0 us
  other arithmetic: 1.7 us -> 0 us
    all_to_all x2 -> x0, blocking collectives: 57.8 us -> none  [the longest x1 34.4 us: on_device(): lax.all_to_all(spectrum, ('lat', 'chan'), split_axis=0, concat_axis=0, ti...]
    pallas_call x3 -> x1, Pallas kernels: 16 us -> 63.8 us  [on_device(): pl.pallas_call(functools.partial(block_kernel, num_lat, num_chan), out_sh...]
    ppermute x2 -> x0, starting transfers between devices: 10.7 us -> none  [the longest x1 8.79 us: on_device(): high = lax.ppermute(turned[:HALO], 'lat', [(i + 1, i) for i in range(ends)])]
    ppermute x2 -> x0, waiting for transfers between devices: 3 us -> none  [the longest x1 2.99 us: on_device(): lax.ppermute(turned[lat_dev - HALO:], 'lat', [(i, i + 1) for i in range(e...]
    concatenate x1 -> x0, other arithmetic: 1.7 us -> none  [on_device(): twice = jnp.concatenate([disco_weight, disco_weight], axis=2)]
    unnamed x4 -> x1, local copies, waits for them, and re-layouts: 0.75 us -> 2.36 us
    slice x1 -> x0, local copies, waits for them, and re-layouts: 1.17 us -> none  [on_device(): high = lax.ppermute(turned[:HALO], 'lat', [(i + 1, i) for i in range(ends)])]
  transfers between devices with their start and end apart: 2 -> 0, of which waited for: 1 -> 0; matrix products, arithmetic and copies ran while one was open for 2% -> 0% of each run, Pallas kernels for 0% -> 0%
where the time goes in v2:
time: 66.4 us; the launch traced here: 66.2 us
  Pallas kernels  63.8 us (96%)
  local copies, waits for them, and re-layouts  2.36 us (4%)
    pallas_call x1, Pallas kernels, on_device(): pl.pallas_call(functools.partial(block_kernel, num_lat, num_chan), out_sh...  63.8 us
    unnamed x1, local copies, waits for them, and re-layouts  2.36 us

profile of v2, /device:TPU:1, one launch (start us, length us, event | category | flops | bytes accessed | tf_op | source)
XLA Modules:
  0.0 66.2 jit_solution(8746871704429183654)
XLA Ops:
  0.0 63.8 %block.1 = bf16[3,384,512]{2,1,0:T(8,128)(2,1)} custom-call(s32[4,9]{1,0:T(4,128)} %shift_lat.1, s32[4,9]{1,0:T(4,128)} %shift_lon.1, s32[4,9]{1,0:T(4,128)} %basis.1, f32[4,9]{1,0:T(4,128)} %value.1, bf16[4,64,1440]{2,1,0:T(8,128)(2,1)} %bitcast.1, bf16[6,64,64]{2,1,0:T(8,128)(2,1)} %weight.1, bf16[256,512]{1,0:T(8,128)(2,1)} %w_up.1, ...), custom_call_target="tpu_custom_call" | custom-call | tf_op jit(solution)/shard_map/block/pallas_call | solution.py:328
  63.8 2.4 %copy.12 = bf16[3,384,512]{2,1,0:T(8,128)(2,1)} copy(bf16[3,384,512]{2,1,0:T(8,128)(2,1)} %block.1) | data formatting | bytes 2359296

commit v3 on v2

--- a/solution.py
+++ b/solution.py
@@ -88,14 +88,18 @@
     shift_lon,
     basis,
     value,
+    fields_hbm,
+    weight_hbm,
+    up_hbm,
+    down_hbm,
+    table_hbm,
+    taken,
     fields,
     weight,
     w_up,
     w_down,
-    table_hbm,
-    legendre_hbm,
-    out,
     own,
+    relay,
     halo,
     ext,
     filters,
@@ -105,14 +109,13 @@
     up,
     down,
     table,
-    legendre,
     total,
     sent,
-    taken,
-    wide,
     load_sem,
     halo_send,
     halo_recv,
+    relay_sent,
+    relay_recv,
     mix_send,
     mix_recv,
     spec_send,
@@ -120,7 +123,6 @@
 ):
     lat_dev, chans, lon_count = fields.shape
     chunks = mixed.shape[1]
-    mode_dev, degrees, lats = legendre.shape
     devices = num_lat * num_chan
     half = lat_dev // 2
     band = lax.axis_index("lat")
@@ -131,12 +133,6 @@
     def device(index):
         return {"lat": lax.div(index, num_chan), "chan": lax.rem(index, num_chan)}
 
-    loads = [
-        pltpu.make_async_copy(table_hbm, table, load_sem.at[0]),
-        pltpu.make_async_copy(legendre_hbm, legendre, load_sem.at[1]),
-    ]
-    for load in loads:
-        load.start()
     barrier = pltpu.get_barrier_semaphore()
 
     def greet(step, carry):
@@ -146,87 +142,158 @@
         return carry
 
     lax.fori_loop(1, devices, greet, 0)
+    pairs = [
+        (fields_hbm, fields),
+        (weight_hbm, weight),
+        (up_hbm, w_up),
+        (down_hbm, w_down),
+        (table_hbm, table),
+    ]
+    loads = [pltpu.make_async_copy(a, b, load_sem.at[i]) for i, (a, b) in enumerate(pairs)]
+    for load in loads:
+        load.start()
     pl.semaphore_wait(barrier, devices - 1)
 
-    upward = pltpu.make_async_remote_copy(
-        src_ref=fields.at[pl.ds(lat_dev - HALO, HALO)],
-        dst_ref=halo.at[0],
-        send_sem=halo_send.at[0],
-        recv_sem=halo_recv.at[0],
-        device_id={"lat": band + 1},
-        device_id_type=MESH,
-    )
-    downward = pltpu.make_async_remote_copy(
-        src_ref=fields.at[pl.ds(0, HALO)],
-        dst_ref=halo.at[1],
-        send_sem=halo_send.at[1],
-        recv_sem=halo_recv.at[1],
-        device_id={"lat": band - 1},
-        device_id_type=MESH,
-    )
-
-    @pl.when(band < num_lat - 1)
+    sends = [
+        [
+            pltpu.make_async_remote_copy(
+                src_ref=fields_hbm.at[lat_dev - 1 - step if side == 0 else step],
+                dst_ref=halo.at[side, HALO - 1 - step if side == 0 else step],
+                send_sem=halo_send.at[side, step],
+                recv_sem=halo_recv.at[side, step],
+                device_id={"lat": band + 1 if side == 0 else band - 1},
+                device_id_type=MESH,
+            )
+            for step in range(HALO)
+        ]
+        for side in range(2)
+    ]
+
+    seam = num_lat // 2
+    ring = seam // 2
+    high_z = lax.div(band, seam)
+    place = lax.rem(lax.div(band, 2), ring)
+    per_lat = ring // HALO
+    width = chans // per_lat
+    at_seam = jnp.logical_or(band == seam - 1, band == seam)
+    is_first = high_z != core
+
+    def part_of(index):
+        return lax.div(index, per_lat), pl.ds(pl.multiple_of(lax.rem(index, per_lat) * width, width), width)
+
+    def relay_send(src, sem, to):
+        return pltpu.make_async_remote_copy(
+            src_ref=src, dst_ref=relay, send_sem=sem, recv_sem=relay_recv,
+            device_id={"lat": to}, device_id_type=MESH,
+        )
+
+    @pl.when(jnp.logical_and(band < num_lat - 1, band != seam - 1))
     def _():
-        upward.start()
-
-    @pl.when(band > 0)
+        for send in sends[0]:
+            send.start()
+
+    @pl.when(jnp.logical_and(band > 0, band != seam))
     def _():
-        downward.start()
-
+        for send in sends[1]:
+            send.start()
+
+    for side, source in ((0, seam - 1), (1, seam)):
+        @pl.when(band == source)
+        def _():
+            def start_part(index, carry):
+                step, rows = part_of(index)
+                to = 2 * index + 1 if side == 0 else seam + 2 * index
+                other = source + seam if side == 0 else source - seam
+                to = jnp.where(to == source, other, to)
+                lat_row = lat_dev - 1 - step if side == 0 else step
+                relay_send(fields_hbm.at[lat_row, rows], halo_send.at[side, step], to).start()
+                return carry
+
+            lax.fori_loop(0, ring, start_part, 0)
+
+    for load in loads[:4]:
+        load.wait()
     for row in range(lat_dev):
         spread(fields[row], ext, HALO + row, lon_count)
         make_filters(row, basis, value, weight, filters)
+    @pl.when(jnp.logical_and(is_first, jnp.logical_not(at_seam)))
+    def _():
+        pltpu.make_async_copy(relay, relay, relay_recv).wait()
+        relay_send(relay, relay_sent, jnp.where(band < seam, band + seam, band - seam)).start()
+
     up[...] = w_up[...].T
     down[...] = w_down[...].T
 
-    def disco_row(row, c):
+    def disco_row(row, to, c):
         start = pl.multiple_of(c * CHUNK, LANES)
         acc = disco_chunk(row, start, shift_lat, shift_lon, ext, filters, columns)
-        here = ext_own[row, :, pl.ds(start, CHUNK)].astype(jnp.float32)
+        here = own[row, :, pl.ds(start, CHUNK)].astype(jnp.float32)
         result = (here + acc).astype(mixed.dtype)
 
-        @pl.when(row == mine)
+        @pl.when(to == mine)
         def _():
             gathered[c, mine] = result
 
-        @pl.when(row != mine)
+        @pl.when(to != mine)
         def _():
-            mixed[row, c] = result
+            mixed[to, c] = result
             pltpu.make_async_remote_copy(
-                src_ref=mixed.at[row, c],
+                src_ref=mixed.at[to, c],
                 dst_ref=gathered.at[c, mine],
                 send_sem=mix_send,
                 recv_sem=mix_recv.at[c],
-                device_id={"chan": row},
+                device_id={"chan": to},
                 device_id_type=MESH,
             ).start()
 
-    ext_own = own
     for row in range(lat_dev):
         own[row, :, :lon_count] = fields[row]
         own[row, :, lon_count:] = jnp.zeros((chans, own.shape[2] - lon_count), own.dtype)
+    first = 1 - core
     for turn in range(2):
-        side = 1 - core if turn == 0 else core
+        side = first if turn == 0 else 1 - first
+        if turn == 1:
+
+            @pl.when(jnp.logical_not(is_first))
+            def _():
+                pltpu.make_async_copy(relay, relay, relay_recv).wait()
+                step, rows = part_of(place)
+                to_side = 1 - core
+                edge = jnp.where(core == 1, HALO - 1 - step, step)
+                pltpu.make_async_remote_copy(
+                    src_ref=relay,
+                    dst_ref=halo.at[to_side, edge, rows],
+                    send_sem=relay_sent,
+                    recv_sem=halo_recv.at[to_side, step],
+                    device_id={"lat": jnp.where(core == 1, seam, seam - 1)},
+                    device_id_type=MESH,
+                ).start()
+
         present = jnp.where(side == 0, band > 0, band < num_lat - 1)
-
-        @pl.when(present)
-        def _():
-            pltpu.make_async_copy(halo.at[side], halo.at[side], halo_recv.at[side]).wait()
-
-        @pl.when(jnp.logical_not(present))
-        def _():
-            halo[side] = jnp.zeros(halo.shape[1:], halo.dtype)
-
-        for r in range(HALO):
-            spread(halo[side, r], ext, side * (HALO + lat_dev) + r, lon_count)
-
-        def steps(step, carry):
-            disco_row(side * half + lax.rem(step, half), lax.div(step, half))
-            return carry
-
-        lax.fori_loop(0, half * chunks, steps, 0)
-
-    loads[0].wait()
+        for step in range(HALO):
+            edge = jnp.where(side == 0, HALO - 1 - step, step)
+            row = jnp.where(side == 0, half - 1 - step, half + step)
+            order = jnp.where(core == 0, step, half - 1 - step)
+            to = order * (num_chan - 1) if turn == 0 else order + 1
+
+            @pl.when(present)
+            def _():
+                arrived = halo.at[side, edge]
+                pltpu.make_async_copy(arrived, arrived, halo_recv.at[side, step]).wait()
+
+            @pl.when(jnp.logical_not(present))
+            def _():
+                halo[side, edge] = jnp.zeros(halo.shape[2:], halo.dtype)
+
+            spread(halo[side, edge], ext, side * (HALO + lat_dev) + edge, lon_count)
+
+            def steps(c, carry):
+                disco_row(row, to, c)
+                return carry
+
+            lax.fori_loop(0, chunks, steps, 0)
+
+    loads[4].wait()
 
     def mlp_part(c):
         pltpu.make_async_copy(
@@ -255,11 +322,17 @@
         piece = total[:, h * LANES : (h + 1) * LANES].astype(jnp.bfloat16)
         sent[:, h * rows : (h + 1) * rows, :] = piece.reshape(devices, rows, LANES)
 
+    at_end = jnp.logical_or(mine == 0, mine == num_chan - 1)
+    order = jnp.where(at_end, lax.div(mine, num_chan - 1), mine - 1)
+    step_here = jnp.where(core == 0, order, half - 1 - order)
+    side_here = jnp.where(at_end, first, 1 - first)
+    lat = band * lat_dev + jnp.where(side_here == 0, half - 1 - step_here, half + step_here)
+
     def hand_out(step, carry):
         to = lax.rem(me + step, devices)
         pltpu.make_async_remote_copy(
             src_ref=sent.at[to],
-            dst_ref=taken.at[me],
+            dst_ref=taken.at[lat],
             send_sem=spec_send,
             recv_sem=spec_recv,
             device_id=device(to),
@@ -268,32 +341,28 @@
         return carry
 
     lax.fori_loop(1, devices, hand_out, 0)
-    taken[me] = sent[me]
-    loads[1].wait()
-    degree = lax.broadcasted_iota(jnp.int32, (degrees, lats), 0)
-    for m in range(mode_dev):
-        kept = jnp.where(degree >= me * mode_dev + m, legendre[m].astype(jnp.float32), 0.0)
-        legendre[m] = kept.astype(jnp.bfloat16)
+    keep = pltpu.make_async_copy(sent.at[me], taken.at[lat], load_sem.at[5])
+    keep.start()
+    keep.wait()
     pltpu.make_async_copy(
         taken.at[pl.ds(0, devices - 1)], taken.at[pl.ds(0, devices - 1)], spec_recv
     ).wait()
-    wide[...] = taken[...].astype(jnp.float32).reshape(devices * PAD, LANES)
-    for m in range(mode_dev):
-        picks = [h * rows + 2 * m + r for r in range(2) for h in range(2)]
-        right = jnp.concatenate(
-            [wide[pl.ds(j, devices, stride=PAD), :].astype(jnp.bfloat16) for j in picks], axis=1
-        )
-        out[m] = jnp.dot(legendre[m], right, preferred_element_type=jnp.float32).astype(out.dtype)
     pltpu.make_async_copy(mixed.at[pl.ds(0, lat_dev - 1)], mixed.at[pl.ds(0, lat_dev - 1)], mix_send).wait()
     pltpu.make_async_copy(sent.at[pl.ds(0, devices - 1)], sent.at[pl.ds(0, devices - 1)], spec_send).wait()
 
+    @pl.when(jnp.logical_not(at_seam))
+    def _():
+        pltpu.make_async_copy(relay, relay, relay_sent).wait()
+
     @pl.when(band < num_lat - 1)
     def _():
-        upward.wait_send()
+        for send in sends[0]:
+            send.wait_send()
 
     @pl.when(band > 0)
     def _():
-        downward.wait_send()
+        for send in sends[1]:
+            send.wait_send()
 
 
 def mlp_chunk(mixed, up, down):
@@ -306,6 +375,35 @@
     active = (0.5 * lifted * (1.0 + jnp.tanh(inner))).astype(jnp.bfloat16)
     lowered = jnp.dot(down, active, preferred_element_type=jnp.float32)
     return (values + lowered).astype(jnp.bfloat16)
+
+
+def legendre_kernel(taken_hbm, legendre_hbm, out_hbm, taken, legendre, out, wide, load_sem, out_sem):
+    mode_dev, degrees, lats = legendre.shape
+    rows = PAD // 2
+    loads = [
+        pltpu.make_async_copy(legendre_hbm, legendre, load_sem.at[0]),
+        pltpu.make_async_copy(taken_hbm, taken, load_sem.at[1]),
+    ]
+    for load in loads:
+        load.start()
+    me = lax.axis_index("lat") * lax.axis_size("chan") + lax.axis_index("chan")
+    degree = lax.broadcasted_iota(jnp.int32, (degrees, lats), 0)
+    loads[0].wait()
+    for m in range(mode_dev):
+        kept = jnp.where(degree >= me * mode_dev + m, legendre[m].astype(jnp.float32), 0.0)
+        legendre[m] = kept.astype(jnp.bfloat16)
+    loads[1].wait()
+    wide[...] = taken[...].astype(jnp.float32).reshape(lats * PAD, LANES)
+    stores = [pltpu.make_async_copy(out.at[m], out_hbm.at[m], out_sem.at[m]) for m in range(mode_dev)]
+    for m in range(mode_dev):
+        picks = [h * rows + 2 * m + r for r in range(2) for h in range(2)]
+        right = jnp.concatenate(
+            [wide[pl.ds(j, lats, stride=PAD), :].astype(jnp.bfloat16) for j in picks], axis=1
+        )
+        out[m] = jnp.dot(legendre[m], right, preferred_element_type=jnp.float32).astype(out.dtype)
+        stores[m].start()
+    for store in stores:
+        store.wait()
 
 
 def on_device(
@@ -320,18 +418,22 @@
     lon_pad = chunks * CHUNK
     hidden = w_up.shape[1]
     smem = pl.BlockSpec(memory_space=pltpu.SMEM)
-    vmem = pl.BlockSpec(memory_space=pltpu.VMEM)
-    hbm = pl.BlockSpec(memory_space=pl.ANY)
+    hbm = pl.BlockSpec(memory_space=pltpu.HBM)
     bf16, f32 = jnp.bfloat16, jnp.float32
     dma = pltpu.SemaphoreType.DMA
     table = jnp.asarray(fourier_rows(lon_count, lon_pad, mode_dev * devices, mode_dev))
-    return pl.pallas_call(
+    taken = pl.pallas_call(
         functools.partial(block_kernel, num_lat, num_chan),
-        out_shape=jax.ShapeDtypeStruct((mode_dev, degrees, 4 * LANES), bf16),
-        in_specs=[smem] * 4 + [vmem] * 4 + [hbm] * 2,
-        out_specs=vmem,
+        out_shape=jax.ShapeDtypeStruct((devices, PAD, LANES), bf16),
+        in_specs=[smem] * 4 + [hbm] * 5,
+        out_specs=hbm,
         scratch_shapes=[
+            pltpu.VMEM((lat_dev, chans, lon_count), bf16),
+            pltpu.VMEM(disco_weight.shape, bf16),
+            pltpu.VMEM(w_up.shape, bf16),
+            pltpu.VMEM(w_down.shape, bf16),
             pltpu.VMEM((lat_dev, chans, lon_pad), bf16),
+            pltpu.VMEM((chans * HALO * 4 // num_lat, lon_count), bf16),
             pltpu.VMEM((2, HALO, chans, lon_count), bf16),
             pltpu.VMEM((lat_dev + 2 * HALO, chans, lon_pad + LANES), f32),
             pltpu.VMEM((lat_dev, G, S * G), bf16),
@@ -341,14 +443,13 @@
             pltpu.VMEM((hidden, num_chan * chans), bf16),
             pltpu.VMEM((num_chan * chans, hidden), bf16),
             pltpu.VMEM(table.shape, bf16),
-            pltpu.VMEM(legendre.shape, bf16),
             pltpu.VMEM((devices * PAD // 2, num_chan * chans), f32),
             pltpu.VMEM((devices, PAD, LANES), bf16),
-            pltpu.VMEM((devices, PAD, LANES), bf16),
-            pltpu.VMEM((devices * PAD, LANES), f32),
-            dma((2,)),
-            dma((2,)),
-            dma((2,)),
+            dma((6,)),
+            dma((2, HALO)),
+            dma((2, HALO)),
+            dma,
+            dma,
             dma,
             dma((chunks,)),
             dma,
@@ -368,8 +469,23 @@
         w_up,
         w_down,
         table,
-        legendre,
     )
+    return pl.pallas_call(
+        legendre_kernel,
+        out_shape=jax.ShapeDtypeStruct((mode_dev, degrees, 4 * LANES), bf16),
+        in_specs=[hbm] * 2,
+        out_specs=hbm,
+        scratch_shapes=[
+            pltpu.VMEM((devices, PAD, LANES), bf16),
+            pltpu.VMEM(legendre.shape, bf16),
+            pltpu.VMEM((mode_dev, degrees, 4 * LANES), bf16),
+            pltpu.VMEM((devices * PAD, LANES), f32),
+            dma((2,)),
+            dma((mode_dev,)),
+        ],
+        compiler_params=pltpu.CompilerParams(vmem_limit_bytes=56 << 20),
+        name="legendre",
+    )(taken, legendre)
 
 
 def solution(mesh):

time: 66.4 us -> 65.7 us (0.989)
  local copies, waits for them, and re-layouts: 2.36 us -> 0 us
  Pallas kernels: 63.8 us -> 65.5 us
    pallas_call x0 -> x1, Pallas kernels: none -> 2.55 us  [on_device(): pl.pallas_call(legendre_kernel, out_shape=jax.ShapeDtypeStruct((mode_dev,...]
    unnamed x1 -> x0, local copies, waits for them, and re-layouts: 2.36 us -> none
    pallas_call x1, Pallas kernels: 63.8 us -> 63 us  [on_device(): pl.pallas_call(functools.partial(block_kernel, num_lat, num_chan), out_sh...]
where the time goes in v3:
time: 65.7 us; the launch traced here: 65.5 us
  Pallas kernels  65.5 us (100%)
    pallas_call x1, Pallas kernels, on_device(): pl.pallas_call(functools.partial(block_kernel, num_lat, num_chan), out_sh...  63 us
    pallas_call x1, Pallas kernels, on_device(): pl.pallas_call(legendre_kernel, out_shape=jax.ShapeDtypeStruct((mode_dev,...  2.55 us

profile of v3, /device:TPU:1, one launch (start us, length us, event | category | flops | bytes accessed | tf_op | source)
XLA Modules:
  0.0 65.5 jit_solution(15457054249206820168)
XLA Ops:
  0.0 63.0 %block.1.taken_hbm = bf16[128,16,128]{2,1,0:T(8,128)(2,1)} custom-call(s32[4,9]{1,0:T(4,128)} %shift_lat.1, s32[4,9]{1,0:T(4,128)} %shift_lon.1, s32[4,9]{1,0:T(4,128)} %basis.1, f32[4,9]{1,0:T(4,128)} %value.1, bf16[4,64,1440]{2,1,0:T(8,128)(2,1)} %bitcast.1, bf16[6,64,64]{2,1,0:T(8,128)(2,1)} %weight_hbm.1, bf16[256,512]{1,0:T(8,128)(2,1)} %up_hbm.1, ...), custom_call_target="tpu_custom_call" | custom-call | tf_op jit(solution)/shard_map/block/pallas_call | solution.py:425
  63.0 2.6 %legendre.1 = bf16[3,384,512]{2,1,0:T(8,128)(2,1)} custom-call(bf16[128,16,128]{2,1,0:T(8,128)(2,1)} %block.1.taken_hbm, bf16[3,384,128]{2,1,0:T(8,128)(2,1)} %legendre_hbm.1), custom_call_target="tpu_custom_call" | custom-call | tf_op jit(solution)/shard_map/legendre/pallas_call | solution.py:473

commit v4 on v3

--- a/solution.py
+++ b/solution.py
@@ -17,7 +17,6 @@
 DLON = 4
 LANES = 128
 CHUNK = 384
-PAD = 16
 MESH = pl.DeviceIdType.MESH
 
 
@@ -27,10 +26,10 @@
     phase = (lon[:, None] * mode[None, :]) % lon_count
     angle = phase.astype(np.float32) * np.float32(2.0 * math.pi / lon_count)
     scale = np.float32(math.sqrt(2.0 / lon_count))
-    table = np.zeros((mode_count // mode_dev, PAD // 2, lon_pad), np.float32)
+    table = np.zeros((2 * mode_dev, mode_count // mode_dev, lon_pad), np.float32)
     pair = np.stack([np.cos(angle), -np.sin(angle)], axis=-1) * scale
     pair = pair.reshape(lon_count, mode_count // mode_dev, 2 * mode_dev)
-    table[:, : 2 * mode_dev, :lon_count] = np.transpose(pair, (1, 2, 0))
+    table[:, :, :lon_count] = np.transpose(pair, (2, 1, 0))
     return table.reshape(-1, lon_pad).astype(ml_dtypes.bfloat16)
 
 
@@ -106,10 +105,13 @@
     columns,
     mixed,
     gathered,
+    rest_mixed,
+    rest,
     up,
     down,
     table,
     total,
+    wide,
     sent,
     load_sem,
     halo_send,
@@ -117,7 +119,10 @@
     relay_sent,
     relay_recv,
     mix_send,
+    last_send,
+    rest_send,
     mix_recv,
+    rest_recv,
     spec_send,
     spec_recv,
 ):
@@ -125,23 +130,28 @@
     chunks = mixed.shape[1]
     devices = num_lat * num_chan
     half = lat_dev // 2
+    per_device = sent.shape[1] * sent.shape[2]
     band = lax.axis_index("lat")
     mine = lax.axis_index("chan")
     me = band * num_chan + mine
     core = lax.rem(band, 2)
 
-    def device(index):
-        return {"lat": lax.div(index, num_chan), "chan": lax.rem(index, num_chan)}
-
     barrier = pltpu.get_barrier_semaphore()
 
-    def greet(step, carry):
+    def greet(band_to, mine_to):
         pl.semaphore_signal(
-            barrier, inc=1, device_id=device(lax.rem(me + step, devices)), device_id_type=MESH
+            barrier, inc=1, device_id={"lat": band_to, "chan": mine_to}, device_id_type=MESH
         )
+
+    for step in range(1, num_chan):
+        greet(band, lax.rem(mine + step, num_chan))
+
+    def greet_band(step, carry):
+        for to in range(num_chan):
+            greet(lax.rem(band + step, num_lat), to)
         return carry
 
-    lax.fori_loop(1, devices, greet, 0)
+    lax.fori_loop(1, num_lat, greet_band, 0)
     pairs = [
         (fields_hbm, fields),
         (weight_hbm, weight),
@@ -211,18 +221,32 @@
 
             lax.fori_loop(0, ring, start_part, 0)
 
-    for load in loads[:4]:
+    for load in loads[:2]:
         load.wait()
     for row in range(lat_dev):
         spread(fields[row], ext, HALO + row, lon_count)
         make_filters(row, basis, value, weight, filters)
-    @pl.when(jnp.logical_and(is_first, jnp.logical_not(at_seam)))
-    def _():
-        pltpu.make_async_copy(relay, relay, relay_recv).wait()
-        relay_send(relay, relay_sent, jnp.where(band < seam, band + seam, band - seam)).start()
-
-    up[...] = w_up[...].T
-    down[...] = w_down[...].T
+
+    left = lon_count % LANES
+    whole = lon_count - (chunks - 1) * CHUNK - left
+    groups = LANES // left
+    tall = chans // groups
+
+    def pack(block):
+        return jnp.concatenate(
+            [block[g * tall : (g + 1) * tall, whole : whole + left] for g in range(groups)], axis=1
+        )
+
+    def unpack(packed):
+        value = packed.astype(jnp.float32)
+        turned = [value] + [pltpu.roll(value, LANES - g * left, 1) for g in range(1, groups)]
+        return jnp.concatenate([t.astype(packed.dtype) for t in turned], axis=0)
+
+    def mix_copy(src, dst, send_sem, recv_sem, to):
+        return pltpu.make_async_remote_copy(
+            src_ref=src, dst_ref=dst, send_sem=send_sem, recv_sem=recv_sem,
+            device_id={"chan": to}, device_id_type=MESH,
+        )
 
     def disco_row(row, to, c):
         start = pl.multiple_of(c * CHUNK, LANES)
@@ -234,17 +258,25 @@
         def _():
             gathered[c, mine] = result
 
+            @pl.when(c == chunks - 1)
+            def _():
+                rest[mine] = pack(result)
+
         @pl.when(to != mine)
         def _():
             mixed[to, c] = result
-            pltpu.make_async_remote_copy(
-                src_ref=mixed.at[to, c],
-                dst_ref=gathered.at[c, mine],
-                send_sem=mix_send,
-                recv_sem=mix_recv.at[c],
-                device_id={"chan": to},
-                device_id_type=MESH,
-            ).start()
+
+            @pl.when(c < chunks - 1)
+            def _():
+                mix_copy(mixed.at[to, c], gathered.at[c, mine], mix_send, mix_recv.at[c], to).start()
+
+            @pl.when(c == chunks - 1)
+            def _():
+                rest_mixed[to] = pack(result)
+                src = mixed.at[to, chunks - 1, :, pl.ds(0, whole)]
+                dst = gathered.at[chunks - 1, mine, :, pl.ds(0, whole)]
+                mix_copy(src, dst, last_send, mix_recv.at[chunks - 1], to).start()
+                mix_copy(rest_mixed.at[to], rest.at[mine], rest_send, rest_recv, to).start()
 
     for row in range(lat_dev):
         own[row, :, :lon_count] = fields[row]
@@ -292,35 +324,49 @@
                 return carry
 
             lax.fori_loop(0, chunks, steps, 0)
-
-    loads[4].wait()
-
-    def mlp_part(c):
-        pltpu.make_async_copy(
-            gathered.at[c, pl.ds(0, num_chan - 1)],
-            gathered.at[c, pl.ds(0, num_chan - 1)],
-            mix_recv.at[c],
-        ).wait()
-        block = gathered[c].reshape(num_chan * chans, CHUNK)
+            if turn == 0 and step == 0:
+
+                @pl.when(jnp.logical_and(is_first, jnp.logical_not(at_seam)))
+                def _():
+                    pltpu.make_async_copy(relay, relay, relay_recv).wait()
+                    relay_send(relay, relay_sent, jnp.where(band < seam, band + seam, band - seam)).start()
+
+    for load in loads[2:5]:
+        load.wait()
+    up[...] = w_up[...].T
+    down[...] = w_down[...].T
+
+    def wait_for(ref, sem):
+        pltpu.make_async_copy(ref, ref, sem).wait()
+
+    def mlp_part(block, c):
         done = mlp_chunk(block, up[...], down[...])
+        wide_lanes = block.shape[1]
         return lax.dot_general(
-            table[:, pl.ds(pl.multiple_of(c * CHUNK, LANES), CHUNK)],
+            table[:, pl.ds(pl.multiple_of(c * CHUNK, LANES), wide_lanes)],
             done,
             (((1,), (1,)), ((), ())),
             preferred_element_type=jnp.float32,
         )
 
-    total[...] = mlp_part(0)
+    total[...] = jnp.zeros(total.shape, total.dtype)
 
     def mlp_step(c, carry):
-        total[...] += mlp_part(c)
+        wait_for(gathered.at[c, pl.ds(0, num_chan - 1)], mix_recv.at[c])
+        total[...] += mlp_part(gathered[c].reshape(num_chan * chans, CHUNK), c)
         return carry
 
-    lax.fori_loop(1, chunks, mlp_step, 0)
-    rows = PAD // 2
-    for h in range(2):
-        piece = total[:, h * LANES : (h + 1) * LANES].astype(jnp.bfloat16)
-        sent[:, h * rows : (h + 1) * rows, :] = piece.reshape(devices, rows, LANES)
+    lax.fori_loop(0, chunks - 1, mlp_step, 0)
+    wait_for(gathered.at[chunks - 1, pl.ds(0, num_chan - 1), :, pl.ds(0, whole)], mix_recv.at[chunks - 1])
+    wait_for(rest.at[pl.ds(0, num_chan - 1)], rest_recv)
+    block = jnp.concatenate([gathered[chunks - 1, p, :, :whole] for p in range(num_chan)], axis=0)
+    tail = jnp.concatenate([unpack(rest[p]) for p in range(num_chan)], axis=0)
+    total[...] += mlp_part(jnp.concatenate([block, tail], axis=1), chunks - 1)
+    for j in range(per_device // 2):
+        for h in range(2):
+            piece = total[j * devices : (j + 1) * devices, h * LANES : (h + 1) * LANES]
+            wide[pl.ds(2 * j + h, devices, stride=per_device), :] = piece
+    sent[...] = wide[...].reshape(sent.shape).astype(sent.dtype)
 
     at_end = jnp.logical_or(mine == 0, mine == num_chan - 1)
     order = jnp.where(at_end, lax.div(mine, num_chan - 1), mine - 1)
@@ -328,26 +374,33 @@
     side_here = jnp.where(at_end, first, 1 - first)
     lat = band * lat_dev + jnp.where(side_here == 0, half - 1 - step_here, half + step_here)
 
-    def hand_out(step, carry):
-        to = lax.rem(me + step, devices)
+    def hand_out(band_to, mine_to):
         pltpu.make_async_remote_copy(
-            src_ref=sent.at[to],
+            src_ref=sent.at[band_to * num_chan + mine_to],
             dst_ref=taken.at[lat],
             send_sem=spec_send,
             recv_sem=spec_recv,
-            device_id=device(to),
+            device_id={"lat": band_to, "chan": mine_to},
             device_id_type=MESH,
         ).start()
+
+    def hand_out_band(step, carry):
+        for to in range(num_chan):
+            hand_out(lax.rem(band + step, num_lat), to)
         return carry
 
-    lax.fori_loop(1, devices, hand_out, 0)
+    lax.fori_loop(1, num_lat, hand_out_band, 0)
+    for step in range(1, num_chan):
+        hand_out(band, lax.rem(mine + step, num_chan))
     keep = pltpu.make_async_copy(sent.at[me], taken.at[lat], load_sem.at[5])
     keep.start()
     keep.wait()
     pltpu.make_async_copy(
         taken.at[pl.ds(0, devices - 1)], taken.at[pl.ds(0, devices - 1)], spec_recv
     ).wait()
-    pltpu.make_async_copy(mixed.at[pl.ds(0, lat_dev - 1)], mixed.at[pl.ds(0, lat_dev - 1)], mix_send).wait()
+    wait_for(mixed.at[pl.ds(0, lat_dev - 1), pl.ds(0, chunks - 1)], mix_send)
+    wait_for(mixed.at[pl.ds(0, lat_dev - 1), chunks - 1, :, pl.ds(0, whole)], last_send)
+    wait_for(rest_mixed.at[pl.ds(0, lat_dev - 1)], rest_send)
     pltpu.make_async_copy(sent.at[pl.ds(0, devices - 1)], sent.at[pl.ds(0, devices - 1)], spec_send).wait()
 
     @pl.when(jnp.logical_not(at_seam))
@@ -379,7 +432,6 @@
 
 def legendre_kernel(taken_hbm, legendre_hbm, out_hbm, taken, legendre, out, wide, load_sem, out_sem):
     mode_dev, degrees, lats = legendre.shape
-    rows = PAD // 2
     loads = [
         pltpu.make_async_copy(legendre_hbm, legendre, load_sem.at[0]),
         pltpu.make_async_copy(taken_hbm, taken, load_sem.at[1]),
@@ -393,12 +445,17 @@
         kept = jnp.where(degree >= me * mode_dev + m, legendre[m].astype(jnp.float32), 0.0)
         legendre[m] = kept.astype(jnp.bfloat16)
     loads[1].wait()
-    wide[...] = taken[...].astype(jnp.float32).reshape(lats * PAD, LANES)
+    wide[...] = taken[...].astype(jnp.float32).reshape(wide.shape)
+    each = wide.shape[0] // lats
+    per_mode = each // mode_dev
     stores = [pltpu.make_async_copy(out.at[m], out_hbm.at[m], out_sem.at[m]) for m in range(mode_dev)]
     for m in range(mode_dev):
-        picks = [h * rows + 2 * m + r for r in range(2) for h in range(2)]
         right = jnp.concatenate(
-            [wide[pl.ds(j, lats, stride=PAD), :].astype(jnp.bfloat16) for j in picks], axis=1
+            [
+                wide[pl.ds(m * per_mode + j, lats, stride=each), :].astype(jnp.bfloat16)
+                for j in range(per_mode)
+            ],
+            axis=1,
         )
         out[m] = jnp.dot(legendre[m], right, preferred_element_type=jnp.float32).astype(out.dtype)
         stores[m].start()
@@ -421,10 +478,12 @@
     hbm = pl.BlockSpec(memory_space=pltpu.HBM)
     bf16, f32 = jnp.bfloat16, jnp.float32
     dma = pltpu.SemaphoreType.DMA
+    packet = (devices, mode_dev, 2 * num_chan * chans // LANES, LANES)
+    packet_rows = packet[0] * packet[1] * packet[2]
     table = jnp.asarray(fourier_rows(lon_count, lon_pad, mode_dev * devices, mode_dev))
     taken = pl.pallas_call(
         functools.partial(block_kernel, num_lat, num_chan),
-        out_shape=jax.ShapeDtypeStruct((devices, PAD, LANES), bf16),
+        out_shape=jax.ShapeDtypeStruct(packet, bf16),
         in_specs=[smem] * 4 + [hbm] * 5,
         out_specs=hbm,
         scratch_shapes=[
@@ -440,18 +499,24 @@
             pltpu.VMEM((S * G, CHUNK), bf16),
             pltpu.VMEM((lat_dev, chunks, chans, CHUNK), bf16),
             pltpu.VMEM((chunks, num_chan, chans, CHUNK), bf16),
+            pltpu.VMEM((lat_dev, chans * (lon_count % LANES) // LANES, LANES), bf16),
+            pltpu.VMEM((num_chan, chans * (lon_count % LANES) // LANES, LANES), bf16),
             pltpu.VMEM((hidden, num_chan * chans), bf16),
             pltpu.VMEM((num_chan * chans, hidden), bf16),
             pltpu.VMEM(table.shape, bf16),
-            pltpu.VMEM((devices * PAD // 2, num_chan * chans), f32),
-            pltpu.VMEM((devices, PAD, LANES), bf16),
+            pltpu.VMEM((2 * mode_dev * devices, num_chan * chans), f32),
+            pltpu.VMEM((packet_rows, LANES), f32),
+            pltpu.VMEM(packet, bf16),
             dma((6,)),
             dma((2, HALO)),
             dma((2, HALO)),
             dma,
             dma,
             dma,
+            dma,
+            dma,
             dma((chunks,)),
+            dma,
             dma,
             dma,
         ],
@@ -472,14 +537,14 @@
     )
     return pl.pallas_call(
         legendre_kernel,
-        out_shape=jax.ShapeDtypeStruct((mode_dev, degrees, 4 * LANES), bf16),
+        out_shape=jax.ShapeDtypeStruct((mode_dev, degrees, 2 * num_chan * chans), bf16),
         in_specs=[hbm] * 2,
         out_specs=hbm,
         scratch_shapes=[
-            pltpu.VMEM((devices, PAD, LANES), bf16),
+            pltpu.VMEM(packet, bf16),
             pltpu.VMEM(legendre.shape, bf16),
-            pltpu.VMEM((mode_dev, degrees, 4 * LANES), bf16),
-            pltpu.VMEM((devices * PAD, LANES), f32),
+            pltpu.VMEM((mode_dev, degrees, 2 * num_chan * chans), bf16),
+            pltpu.VMEM((packet_rows, LANES), f32),
             dma((2,)),
             dma((mode_dev,)),
         ],

time: 65.7 us -> 61.1 us (0.930)
  Pallas kernels: 65.5 us -> 60.9 us
    pallas_call x1, Pallas kernels: 63 us -> 58.5 us  [on_device(): pl.pallas_call(functools.partial(block_kernel, num_lat, num_chan), out_sh...]
where the time goes in v4:
time: 61.1 us; the launch traced here: 60.9 us
  Pallas kernels  60.9 us (100%)
    pallas_call x1, Pallas kernels, on_device(): pl.pallas_call(functools.partial(block_kernel, num_lat, num_chan), out_sh...  58.5 us
    pallas_call x1, Pallas kernels, on_device(): pl.pallas_call(legendre_kernel, out_shape=jax.ShapeDtypeStruct((mode_dev,...  2.46 us

profile of v4, /device:TPU:1, one launch (start us, length us, event | category | flops | bytes accessed | tf_op | source)
XLA Modules:
  0.0 60.9 jit_solution(4564944000097289822)
XLA Ops:
  0.0 58.5 %block.1.taken_hbm = bf16[128,3,4,128]{3,2,1,0:T(4,128)(2,1)} custom-call(s32[4,9]{1,0:T(4,128)} %shift_lat.1, s32[4,9]{1,0:T(4,128)} %shift_lon.1, s32[4,9]{1,0:T(4,128)} %basis.1, f32[4,9]{1,0:T(4,128)} %value.1, bf16[4,64,1440]{2,1,0:T(8,128)(2,1)} %bitcast.1, bf16[6,64,64]{2,1,0:T(8,128)(2,1)} %weight_hbm.1, bf16[256,512]{1,0:T(8,128)(2,1)} %up_hbm.1, ...), custom_call_target="tpu_custom_call" | custom-call | tf_op jit(solution)/shard_map/block/pallas_call | solution.py:484
  58.5 2.5 %legendre.1 = bf16[3,384,512]{2,1,0:T(8,128)(2,1)} custom-call(bf16[128,3,4,128]{3,2,1,0:T(4,128)(2,1)} %block.1.taken_hbm, bf16[3,384,128]{2,1,0:T(8,128)(2,1)} %legendre_hbm.1), custom_call_target="tpu_custom_call" | custom-call | tf_op jit(solution)/shard_map/legendre/pallas_call | solution.py:538

commit v5 on v4

--- a/solution.py
+++ b/solution.py
@@ -136,22 +136,6 @@
     me = band * num_chan + mine
     core = lax.rem(band, 2)
 
-    barrier = pltpu.get_barrier_semaphore()
-
-    def greet(band_to, mine_to):
-        pl.semaphore_signal(
-            barrier, inc=1, device_id={"lat": band_to, "chan": mine_to}, device_id_type=MESH
-        )
-
-    for step in range(1, num_chan):
-        greet(band, lax.rem(mine + step, num_chan))
-
-    def greet_band(step, carry):
-        for to in range(num_chan):
-            greet(lax.rem(band + step, num_lat), to)
-        return carry
-
-    lax.fori_loop(1, num_lat, greet_band, 0)
     pairs = [
         (fields_hbm, fields),
         (weight_hbm, weight),
@@ -162,6 +146,22 @@
     loads = [pltpu.make_async_copy(a, b, load_sem.at[i]) for i, (a, b) in enumerate(pairs)]
     for load in loads:
         load.start()
+    barrier = pltpu.get_barrier_semaphore()
+
+    def greet(band_to, mine_to):
+        pl.semaphore_signal(
+            barrier, inc=1, device_id={"lat": band_to, "chan": mine_to}, device_id_type=MESH
+        )
+
+    for step in range(1, num_chan):
+        greet(band, lax.rem(mine + step, num_chan))
+
+    def greet_band(step, carry):
+        for to in range(num_chan):
+            greet(lax.rem(band + step, num_lat), to)
+        return carry
+
+    lax.fori_loop(1, num_lat, greet_band, 0)
     pl.semaphore_wait(barrier, devices - 1)
 
     sends = [
@@ -210,7 +210,10 @@
     for side, source in ((0, seam - 1), (1, seam)):
         @pl.when(band == source)
         def _():
-            def start_part(index, carry):
+            def start_part(count, carry):
+                pace = lax.div(count, 2)
+                index = jnp.where(lax.rem(count, 2) == 0, ring // 2 + pace, ring // 2 - 1 - pace)
+                index = ring - 1 - index if side == 0 else index
                 step, rows = part_of(index)
                 to = 2 * index + 1 if side == 0 else seam + 2 * index
                 other = source + seam if side == 0 else source - seam
@@ -225,7 +228,11 @@
         load.wait()
     for row in range(lat_dev):
         spread(fields[row], ext, HALO + row, lon_count)
-        make_filters(row, basis, value, weight, filters)
+
+    @pl.when(jnp.logical_and(is_first, jnp.logical_not(at_seam)))
+    def _():
+        pltpu.make_async_copy(relay, relay, relay_recv).wait()
+        relay_send(relay, relay_sent, jnp.where(band < seam, band + seam, band - seam)).start()
 
     left = lon_count % LANES
     whole = lon_count - (chunks - 1) * CHUNK - left
@@ -284,27 +291,11 @@
     first = 1 - core
     for turn in range(2):
         side = first if turn == 0 else 1 - first
-        if turn == 1:
-
-            @pl.when(jnp.logical_not(is_first))
-            def _():
-                pltpu.make_async_copy(relay, relay, relay_recv).wait()
-                step, rows = part_of(place)
-                to_side = 1 - core
-                edge = jnp.where(core == 1, HALO - 1 - step, step)
-                pltpu.make_async_remote_copy(
-                    src_ref=relay,
-                    dst_ref=halo.at[to_side, edge, rows],
-                    send_sem=relay_sent,
-                    recv_sem=halo_recv.at[to_side, step],
-                    device_id={"lat": jnp.where(core == 1, seam, seam - 1)},
-                    device_id_type=MESH,
-                ).start()
-
         present = jnp.where(side == 0, band > 0, band < num_lat - 1)
         for step in range(HALO):
             edge = jnp.where(side == 0, HALO - 1 - step, step)
             row = jnp.where(side == 0, half - 1 - step, half + step)
+            make_filters(row, basis, value, weight, filters)
             order = jnp.where(core == 0, step, half - 1 - step)
             to = order * (num_chan - 1) if turn == 0 else order + 1
 
@@ -324,12 +315,22 @@
                 return carry
 
             lax.fori_loop(0, chunks, steps, 0)
-            if turn == 0 and step == 0:
-
-                @pl.when(jnp.logical_and(is_first, jnp.logical_not(at_seam)))
+            if turn == 1 and step == 0:
+
+                @pl.when(jnp.logical_not(is_first))
                 def _():
                     pltpu.make_async_copy(relay, relay, relay_recv).wait()
-                    relay_send(relay, relay_sent, jnp.where(band < seam, band + seam, band - seam)).start()
+                    relay_step, rows = part_of(place)
+                    to_side = 1 - core
+                    relay_edge = jnp.where(core == 1, HALO - 1 - relay_step, relay_step)
+                    pltpu.make_async_remote_copy(
+                        src_ref=relay,
+                        dst_ref=halo.at[to_side, relay_edge, rows],
+                        send_sem=relay_sent,
+                        recv_sem=halo_recv.at[to_side, relay_step],
+                        device_id={"lat": jnp.where(core == 1, seam, seam - 1)},
+                        device_id_type=MESH,
+                    ).start()
 
     for load in loads[2:5]:
         load.wait()

time: 61.1 us -> 59.2 us (0.969)
  Pallas kernels: 60.9 us -> 59.1 us
    pallas_call x1, Pallas kernels: 58.5 us -> 56.6 us  [on_device(): pl.pallas_call(functools.partial(block_kernel, num_lat, num_chan), out_sh...]
where the time goes in v5:
time: 59.2 us; the launch traced here: 59.1 us
  Pallas kernels  59.1 us (100%)
    pallas_call x1, Pallas kernels, on_device(): pl.pallas_call(functools.partial(block_kernel, num_lat, num_chan), out_sh...  56.6 us
    pallas_call x1, Pallas kernels, on_device(): pl.pallas_call(legendre_kernel, out_shape=jax.ShapeDtypeStruct((mode_dev,...  2.46 us

profile of v5, /device:TPU:1, one launch (start us, length us, event | category | flops | bytes accessed | tf_op | source)
XLA Modules:
  0.0 59.1 jit_solution(2290815879179433546)
XLA Ops:
  0.0 56.6 %block.1.taken_hbm = bf16[128,3,4,128]{3,2,1,0:T(4,128)(2,1)} custom-call(s32[4,9]{1,0:T(4,128)} %shift_lat.1, s32[4,9]{1,0:T(4,128)} %shift_lon.1, s32[4,9]{1,0:T(4,128)} %basis.1, f32[4,9]{1,0:T(4,128)} %value.1, bf16[4,64,1440]{2,1,0:T(8,128)(2,1)} %bitcast.1, bf16[6,64,64]{2,1,0:T(8,128)(2,1)} %weight_hbm.1, bf16[256,512]{1,0:T(8,128)(2,1)} %up_hbm.1, ...), custom_call_target="tpu_custom_call" | custom-call | tf_op jit(solution)/shard_map/block/pallas_call | solution.py:485
  56.6 2.5 %legendre.1 = bf16[3,384,512]{2,1,0:T(8,128)(2,1)} custom-call(bf16[128,3,4,128]{3,2,1,0:T(4,128)(2,1)} %block.1.taken_hbm, bf16[3,384,128]{2,1,0:T(8,128)(2,1)} %legendre_hbm.1), custom_call_target="tpu_custom_call" | custom-call | tf_op jit(solution)/shard_map/legendre/pallas_call | solution.py:539

commit v6 on v5

--- a/solution.py
+++ b/solution.py
@@ -386,8 +386,8 @@
         ).start()
 
     def hand_out_band(step, carry):
-        for to in range(num_chan):
-            hand_out(lax.rem(band + step, num_lat), to)
+        for turn in range(num_chan):
+            hand_out(lax.rem(band + step, num_lat), lax.rem(mine + turn, num_chan))
         return carry
 
     lax.fori_loop(1, num_lat, hand_out_band, 0)

time: 59.2 us -> 59.3 us (level)
  no operation moved by 1% of the time
where the time goes in v6:
time: 59.3 us; the launch traced here: 59.1 us
  Pallas kernels  59.1 us (100%)
    pallas_call x1, Pallas kernels, on_device(): pl.pallas_call(functools.partial(block_kernel, num_lat, num_chan), out_sh...  56.6 us
    pallas_call x1, Pallas kernels, on_device(): pl.pallas_call(legendre_kernel, out_shape=jax.ShapeDtypeStruct((mode_dev,...  2.46 us

profile of v6, /device:TPU:1, one launch (start us, length us, event | category | flops | bytes accessed | tf_op | source)
XLA Modules:
  0.0 59.1 jit_solution(14903591678670012686)
XLA Ops:
  0.0 56.6 %block.1.taken_hbm = bf16[128,3,4,128]{3,2,1,0:T(4,128)(2,1)} custom-call(s32[4,9]{1,0:T(4,128)} %shift_lat.1, s32[4,9]{1,0:T(4,128)} %shift_lon.1, s32[4,9]{1,0:T(4,128)} %basis.1, f32[4,9]{1,0:T(4,128)} %value.1, bf16[4,64,1440]{2,1,0:T(8,128)(2,1)} %bitcast.1, bf16[6,64,64]{2,1,0:T(8,128)(2,1)} %weight_hbm.1, bf16[256,512]{1,0:T(8,128)(2,1)} %up_hbm.1, ...), custom_call_target="tpu_custom_call" | custom-call | tf_op jit(solution)/shard_map/block/pallas_call | solution.py:485
  56.7 2.5 %legendre.1 = bf16[3,384,512]{2,1,0:T(8,128)(2,1)} custom-call(bf16[128,3,4,128]{3,2,1,0:T(4,128)(2,1)} %block.1.taken_hbm, bf16[3,384,128]{2,1,0:T(8,128)(2,1)} %legendre_hbm.1), custom_call_target="tpu_custom_call" | custom-call | tf_op jit(solution)/shard_map/legendre/pallas_call | solution.py:539
